TPU v7x, 32 devices: a whole 2x2x4 slice. The times are simulated.
32 devices in a mesh: blk: 8 (over y, x, core), head: 4 (over z).
Axes of the slice: x: 2, y: 2, z: 4, core: 2. Of those that a mesh axis runs over, the one named last changes fastest.
Arguments:
- query: bfloat16 [4096, 8192], P(('blk', 'head')), may hold values from -6 to 6
- key: bfloat16 [4096, 1024], P(('blk', 'head')), may hold values from -6 to 6
- value: bfloat16 [4096, 1024], P(('blk', 'head')), may hold values from -6 to 6
- output: bfloat16 [4096, 8192], P(('blk', 'head')), may hold values from -1.5 to 1.5
- out_grad: bfloat16 [4096, 8192], P(('blk', 'head')), may hold values from -6 to 6
- lse: float32 [4096, 64], P(('blk', 'head')), may hold values from 3.5 to 6
- doc_lengths: int32 [3], replicated, may hold values from 1 to 2048, as said below
- block_keep: int32 [32, 17], P('blk'), may hold values 0 or 1
Outputs:
- query_grad: bfloat16 [4096, 8192], P(('blk', 'head'))
- key_grad: bfloat16 [4096, 1024], P(('blk', 'head'))
- value_grad: bfloat16 [4096, 1024], P(('blk', 'head'))
Inputs may be any that keep to these rules, and one draw needn't show every extreme that they name: `doc_lengths`: whole document lengths that sum to 4096; the sequence is cut into aligned windows of 2048 tokens, each but the last split into two documents, the last one document of exactly 2048.
All inputs are finite; a program needn't handle non-finite values. No bound on the sum of `block_keep` on one device may be relied on, other than what follows from the above.
Results may differ from a plain program's by a relative error of at most 0.015.
Values may be sent and summed in bfloat16 or wider, within the bound.
A program may use at most 128 MiB of HBM per device.

v0:
```python
import math

import jax
import jax.numpy as jnp
from jax import lax
from jax.sharding import PartitionSpec as P

KVH = 8
HD = 128
DOC_MAX = 2048
BLOCK = 128


def from_behind(value, axis, by):
    length = lax.axis_size(axis)
    pairs = [(i, i + by) for i in range(length) if 0 <= i + by < length]
    return lax.ppermute(value, axis, pairs)


def passed_along(value, axis, by):
    length = lax.axis_size(axis)
    return lax.ppermute(value, axis, [(i, (i + by) % length) for i in range(length)])


def for_sending(value):
    return jax.tree.map(lambda a: a.astype(jnp.bfloat16) if a.dtype == jnp.float32 else a, value)


def doc_index(positions, starts):
    return jnp.sum((positions[:, None] >= starts[None, :]).astype(jnp.int32), axis=1) - 1


def block_table(first_query, first_key, rows, count_query, count_key):
    query_blocks = first_query // BLOCK + jnp.arange(count_query // BLOCK, dtype=jnp.int32)
    key_blocks = first_key // BLOCK + jnp.arange(count_key // BLOCK, dtype=jnp.int32)
    distance = query_blocks[:, None] - key_blocks[None, :]
    offsets = jnp.arange(rows.shape[1], dtype=jnp.int32)
    table = (
        jnp.sum(
            jnp.where(distance[:, :, None] == offsets[None, None, :], rows[:, None, :], 0), axis=2
        )
        > 0
    )
    return jnp.repeat(jnp.repeat(table, BLOCK, axis=0), BLOCK, axis=1)


def piece_grads(q_group, g_group, lse_group, delta_group, keys, values, allowed, scale):
    f32 = jnp.float32
    scores = jnp.einsum("tcgd,scd->cgts", q_group, keys, preferred_element_type=f32) * scale
    probs = jnp.where(allowed[None, None], jnp.exp(scores - lse_group[..., None]), 0.0)
    dprobs = jnp.einsum("tcgd,scd->cgts", g_group, values, preferred_element_type=f32)
    dscores = probs * (dprobs - delta_group[..., None])
    probs_b = probs.astype(jnp.bfloat16)
    dscores_b = dscores.astype(jnp.bfloat16)
    dv_part = jnp.einsum("cgts,tcgd->scd", probs_b, g_group, preferred_element_type=f32)
    dk_part = jnp.einsum("cgts,tcgd->scd", dscores_b, q_group, preferred_element_type=f32)
    dq_part = jnp.einsum("cgts,scd->tcgd", dscores_b, keys, preferred_element_type=f32)
    return (dq_part, dk_part, dv_part)


def shards(query, key, value, output, out_grad, lse, doc_lengths, block_keep):
    f32 = jnp.float32
    heads_axis = lax.axis_size("head")
    repeat = max(1, heads_axis // KVH)
    local_rows = query.shape[0]
    scale = 1.0 / math.sqrt(HD)
    q_range, o_range, g_range = (
        lax.all_to_all(query, "head", split_axis=1, concat_axis=0, tiled=True),
        lax.all_to_all(output, "head", split_axis=1, concat_axis=0, tiled=True),
        lax.all_to_all(out_grad, "head", split_axis=1, concat_axis=0, tiled=True),
    )
    lse_range = lax.all_to_all(lse, "head", split_axis=1, concat_axis=0, tiled=True)
    width = q_range.shape[1] // HD
    delta_range = jnp.sum(
        g_range.reshape(-1, width, HD).astype(f32) * o_range.reshape(-1, width, HD).astype(f32),
        axis=2,
    )
    key_rep = jnp.repeat(key.reshape(local_rows, KVH, HD), repeat, axis=1).reshape(
        local_rows, KVH * repeat * HD
    )
    value_rep = jnp.repeat(value.reshape(local_rows, KVH, HD), repeat, axis=1).reshape(
        local_rows, KVH * repeat * HD
    )
    key_range, value_range = (
        lax.all_to_all(key_rep, "head", split_axis=1, concat_axis=0, tiled=True),
        lax.all_to_all(value_rep, "head", split_axis=1, concat_axis=0, tiled=True),
    )
    range_rows = q_range.shape[0]
    local_heads = q_range.shape[1] // HD
    local_kv = key_range.shape[1] // HD
    group = local_heads // local_kv
    q_group = q_range.reshape(range_rows, local_kv, group, HD)
    g_group = g_range.reshape(range_rows, local_kv, group, HD)
    lse_group = lse_range.reshape(range_rows, local_kv, group).transpose(1, 2, 0)
    delta_group = delta_range.reshape(range_rows, local_kv, group).transpose(1, 2, 0)
    keys_own = key_range.reshape(range_rows, local_kv, HD)
    values_own = value_range.reshape(range_rows, local_kv, HD)
    starts = jnp.cumsum(doc_lengths) - doc_lengths
    position = lax.axis_index("blk")
    first_query = position * range_rows
    q_pos = first_query + jnp.arange(range_rows, dtype=jnp.int32)
    q_doc = doc_index(q_pos, starts)

    def allowed_for(first_key):
        k_pos = first_key + jnp.arange(range_rows, dtype=jnp.int32)
        same = q_doc[:, None] == doc_index(k_pos, starts)[None, :]
        causal = k_pos[None, :] <= q_pos[:, None]
        return (
            same & causal & block_table(first_query, first_key, block_keep, range_rows, range_rows)
        )

    reach = DOC_MAX // range_rows
    half = range_rows // 2
    own_allowed = allowed_for(first_query)
    dq_upper, dk_upper, dv_upper = piece_grads(
        q_group[:half],
        g_group[:half],
        lse_group[..., :half],
        delta_group[..., :half],
        keys_own[:half],
        values_own[:half],
        own_allowed[:half, :half],
        scale,
    )
    dq_lower, dk_lower, dv_lower = piece_grads(
        q_group[half:],
        g_group[half:],
        lse_group[..., half:],
        delta_group[..., half:],
        keys_own,
        values_own,
        own_allowed[half:],
        scale,
    )
    dq_total = jnp.concatenate([dq_upper, dq_lower], axis=0)
    filler = jnp.zeros((range_rows - half,) + dk_upper.shape[1:], f32)
    dk_home = dk_lower + jnp.concatenate([dk_upper, filler], axis=0)
    dv_home = dv_lower + jnp.concatenate([dv_upper, filler], axis=0)
    moving = (keys_own, values_own)
    carried = (dk_home, dv_home)
    for step in range(1, reach + 1):
        moving = from_behind((moving[0], moving[1]), "blk", 1)
        carried = passed_along((carried[0], carried[1]), "blk", 1)
        dq_part, dk_part, dv_part = piece_grads(
            q_group,
            g_group,
            lse_group,
            delta_group,
            moving[0],
            moving[1],
            allowed_for((position - step) * range_rows),
            scale,
        )
        dq_total = dq_total + dq_part
        carried = (carried[0] + dk_part, carried[1] + dv_part)
    dk_final, dv_final = (
        passed_along(carried[0].astype(jnp.bfloat16), "blk", -reach).astype(jnp.float32),
        passed_along(carried[1].astype(jnp.bfloat16), "blk", -reach).astype(jnp.float32),
    )
    dk_rows = (dk_final * scale).reshape(range_rows, local_kv * HD)
    dv_rows = dv_final.reshape(range_rows, local_kv * HD)
    dk_back, dv_back = (
        lax.all_to_all(
            for_sending(dk_rows), "head", split_axis=0, concat_axis=1, tiled=True
        ).astype(dk_rows.dtype),
        lax.all_to_all(
            for_sending(dv_rows), "head", split_axis=0, concat_axis=1, tiled=True
        ).astype(dv_rows.dtype),
    )
    key_grad = jnp.sum(dk_back.reshape(local_rows, KVH, repeat, HD), axis=2).reshape(
        local_rows, KVH * HD
    )
    value_grad = jnp.sum(dv_back.reshape(local_rows, KVH, repeat, HD), axis=2).reshape(
        local_rows, KVH * HD
    )
    dq_rows = (dq_total * scale).astype(jnp.bfloat16).reshape(range_rows, local_heads * HD)
    query_grad = lax.all_to_all(dq_rows, "head", split_axis=0, concat_axis=1, tiled=True)
    return (query_grad, key_grad.astype(jnp.bfloat16), value_grad.astype(jnp.bfloat16))


def solution(mesh):
    in_specs = (
        P(("blk", "head"), None),
        P(("blk", "head"), None),
        P(("blk", "head"), None),
        P(("blk", "head"), None),
        P(("blk", "head"), None),
        P(("blk", "head"), None),
        P(),
        P("blk", None),
    )
    out_specs = (P(("blk", "head"), None), P(("blk", "head"), None), P(("blk", "head"), None))
    return jax.shard_map(shards, mesh=mesh, in_specs=in_specs, out_specs=out_specs, check_vma=False)
```

profile of v0, /device:TPU:0, one launch (start us, length us, event | category | flops | bytes accessed | tf_op | source)
XLA Modules:
  0.0 504.3 jit_solution(5930566282033421794)
XLA Ops:
  0.6 6.3 %all-to-all-start.2 = ((f32[128,4,16]{0,2,1:T(8,128)}), f32[128,4,16]{0,2,1:T(8,128)S(1)}, u32[]{:S(2)}, u32[]{:S(2)}) async-start(f32[128,4,16]{0,2,1:T(8,128)} %bitcast.459), calls=%async_computation.2 | async-start | bytes 65536 | tf_op jit(solution)/shard_map/all_to_all | solution.py:72
  17.7 6.2 %all-to-all-done = bf16[128,4,256]{2,0,1:T(8,128)(2,1)S(1)} async-done(((bf16[128,4,256]{2,0,1:T(8,128)(2,1)}), bf16[128,4,256]{2,0,1:T(8,128)(2,1)S(1)}, u32[]{:S(2)}, u32[]{:S(2)}) %all-to-all-start) | async-done | bytes 262176 | tf_op jit(solution)/shard_map/all_to_all | solution.py:85
  40.9 41.8 %all-to-all-done.1 = bf16[128,4,2048]{2,0,1:T(8,128)(2,1)S(1)} async-done(((bf16[128,4,2048]{2,0,1:T(8,128)(2,1)}), bf16[128,4,2048]{2,0,1:T(8,128)(2,1)S(1)}, u32[]{:S(2)}, u32[]{:S(2)}) %all-to-all-start.1) | async-done | bytes 2097184 | tf_op jit(solution)/shard_map/all_to_all | solution.py:68
  91.5 43.7 %all-to-all-done.4 = bf16[128,4,2048]{2,0,1:T(8,128)(2,1)S(1)} async-done(((bf16[128,4,2048]{2,0,1:T(8,128)(2,1)}), bf16[128,4,2048]{2,0,1:T(8,128)(2,1)S(1)}, u32[]{:S(2)}, u32[]{:S(2)}) %all-to-all-start.4) | async-done | bytes 2097184 | tf_op jit(solution)/shard_map/all_to_all | solution.py:70
  135.2 4.5 all-to-all-start.5
  159.2 4.4 collective-permute-start.4
  171.1 4.4 collective-permute-start.6
  179.7 7.7 %all-to-all-done.5 = bf16[128,4,2048]{2,0,1:T(8,128)(2,1)} async-done(((bf16[128,4,2048]{2,0,1:T(8,128)(2,1)}), bf16[128,4,2048]{2,0,1:T(8,128)(2,1)}, u32[]{:S(2)}, u32[]{:S(2)}) %all-to-all-start.5) | async-done | bytes 2097184 | tf_op jit(solution)/shard_map/all_to_all | solution.py:69
  216.6 8.1 %fusion.105 = f32[2,512,512,8]{2,1,3,0:T(8,128)} fusion(bf16[512,2,8,128]{3,2,1,0:T(8,128)(2,1)S(1)} %bitcast.382, bf16[512,2,128]{2,0,1:T(8,128)(2,1)S(1)} %collective-permute-done.2), kind=kOutput, calls=%fused_computation.116 | convolution fusion | flops 1073741824 | bytes 19136512 | tf_op jit(solution)/shard_map/tcgd,scd->cgts/dot_general | solution.py:49
  224.8 10.4 %fusion.59 = f32[512,2,128]{2,0,1:T(8,128)} fusion(f32[2,512,512,8]{2,1,3,0:T(8,128)} %fusion.105, f32[2,8,512]{2,1,0:T(8,128)S(1)} %bitcast.451, pred[512,512]{0,1:T(8,128)(4,1)S(1)} %copy-done.14, bf16[512,2,8,128]{3,2,1,0:T(8,128)(2,1)} %bitcast.418), kind=kOutput, calls=%fused_computation.73 | convolution fusion | flops 1090519040 | bytes 19693568 | tf_op jit(solution)/shard_map/cgts,tcgd->scd/dot_general | solution.py:55
  235.1 9.1 %fusion.103 = f32[2,512,512,8]{2,1,3,0:T(8,128)} fusion(bf16[512,2,8,128]{3,2,1,0:T(8,128)(2,1)S(1)} %bitcast.383, bf16[512,2,128]{2,0,1:T(8,128)(2,1)} %collective-permute-done.4), kind=kOutput, calls=%fused_computation.114 | convolution fusion | flops 1073741824 | bytes 19136512 | tf_op jit(solution)/shard_map/tcgd,scd->cgts/dot_general | solution.py:49
  244.2 9.2 %fusion.62 = f32[512,2,128]{2,0,1:T(8,128)S(1)} fusion(f32[2,512,512,8]{2,1,3,0:T(8,128)} %fusion.103, f32[2,8,512]{2,1,0:T(8,128)S(1)} %bitcast.452, pred[512,512]{0,1:T(8,128)(4,1)} %get-tuple-element.35, bf16[512,2,8,128]{3,2,1,0:T(8,128)(2,1)} %bitcast.419), kind=kOutput, calls=%fused_computation.74 | convolution fusion | flops 1090519040 | bytes 19693568 | tf_op jit(solution)/shard_map/cgts,tcgd->scd/dot_general | solution.py:55
  253.5 8.1 %fusion.101 = f32[2,512,512,8]{2,1,3,0:T(8,128)} fusion(bf16[512,2,8,128]{3,2,1,0:T(8,128)(2,1)S(1)} %bitcast.384, bf16[512,2,128]{2,0,1:T(8,128)(2,1)S(1)} %collective-permute-done.6), kind=kOutput, calls=%fused_computation.112 | convolution fusion | flops 1073741824 | bytes 19136512 | tf_op jit(solution)/shard_map/tcgd,scd->cgts/dot_general | solution.py:49
  261.6 10.5 %fusion.65 = f32[512,2,128]{2,0,1:T(8,128)} fusion(f32[2,512,512,8]{2,1,3,0:T(8,128)} %fusion.101, f32[2,8,512]{2,1,0:T(8,128)S(1)} %bitcast.453, pred[512,512]{0,1:T(8,128)(4,1)} %get-tuple-element.33, bf16[512,2,8,128]{3,2,1,0:T(8,128)(2,1)} %bitcast.420), kind=kOutput, calls=%fused_computation.75 | convolution fusion | flops 1090519040 | bytes 19693568 | tf_op jit(solution)/shard_map/cgts,tcgd->scd/dot_general | solution.py:55
  272.0 11.3 %fusion.9 = bf16[2,8,512,512]{2,3,1,0:T(8,128)(2,1)} fusion(f32[2,512,512,8]{2,1,3,0:T(8,128)} %fusion.105, f32[2,8,512]{2,1,0:T(8,128)S(1)} %bitcast.446, f32[2,8,512]{2,1,0:T(8,128)S(1)} %bitcast.454, pred[512,512]{0,1:T(8,128)(4,1)} %get-tuple-element.34, bf16[512,2,8,128]{3,2,1,0:T(8,128)(2,1)} %bitcast.421, bf16[512,2,128]{2,0,1:T(8,128)(2,1)} %collective-permute-done.3), kind=kOutput, calls=%fused_computation.14 | convolution fusion | flops 1098907648 | bytes 27852800 | tf_op jit(solution)/shard_map/tcgd,scd->cgts/dot_general | solution.py:51
  283.4 10.0 %fusion.5 = bf16[2,8,512,512]{2,3,1,0:T(8,128)(2,1)S(1)} fusion(f32[2,512,512,8]{2,1,3,0:T(8,128)} %fusion.103, f32[2,8,512]{2,1,0:T(8,128)S(1)} %bitcast.447, f32[2,8,512]{2,1,0:T(8,128)S(1)} %bitcast.455, pred[512,512]{0,1:T(8,128)(4,1)S(1)} %copy-done.13, bf16[512,2,8,128]{3,2,1,0:T(8,128)(2,1)} %bitcast.422, bf16[512,2,128]{2,0,1:T(8,128)(2,1)} %collective-permute-done.5), kind=kOutput, calls=%fused_computation.8 | convolution fusion | flops 1098907648 | bytes 27852800 | tf_op jit(solution)/shard_map/tcgd,scd->cgts/dot_general | solution.py:51
  293.3 11.8 %fusion.117 = f32[2,8,512,128]{3,2,1,0:T(8,128)} fusion(bf16[2,8,512,512]{2,3,1,0:T(8,128)(2,1)} %fusion.9, bf16[512,2,128]{2,0,1:T(8,128)(2,1)S(1)} %collective-permute-done.2), kind=kOutput, calls=%fused_computation.130 | convolution fusion | flops 1073741824 | bytes 12845056 | tf_op jit(solution)/shard_map/cgts,scd->tcgd/dot_general | solution.py:57
  305.1 6.5 %fusion.113 = f32[2,8,512,128]{3,2,1,0:T(8,128)} fusion(bf16[2,8,512,512]{2,3,1,0:T(8,128)(2,1)S(1)} %fusion.5, bf16[512,2,128]{2,0,1:T(8,128)(2,1)} %collective-permute-done.4), kind=kOutput, calls=%fused_computation.126 | convolution fusion | flops 1073741824 | bytes 12845056 | tf_op jit(solution)/shard_map/cgts,scd->tcgd/dot_general | solution.py:57
  311.6 8.2 %fusion.107 = f32[2,512,512,8]{2,1,3,0:T(8,128)} fusion(bf16[512,2,8,128]{3,2,1,0:T(8,128)(2,1)S(1)} %bitcast.385, bf16[512,2,128]{2,0,1:T(8,128)(2,1)S(1)} %collective-permute-done), kind=kOutput, calls=%fused_computation.118 | convolution fusion | flops 1073741824 | bytes 19136512 | tf_op jit(solution)/shard_map/tcgd,scd->cgts/dot_general | solution.py:49
  319.8 11.4 %fusion.1 = bf16[2,8,512,512]{2,3,1,0:T(8,128)(2,1)} fusion(f32[2,512,512,8]{2,1,3,0:T(8,128)} %fusion.101, f32[2,8,512]{2,1,0:T(8,128)S(1)} %bitcast.448, f32[2,8,512]{2,1,0:T(8,128)S(1)} %bitcast.456, pred[512,512]{0,1:T(8,128)(4,1)S(1)} %copy-done.12, bf16[512,2,8,128]{3,2,1,0:T(8,128)(2,1)S(1)} %bitcast.425, bf16[512,2,128]{2,0,1:T(8,128)(2,1)} %collective-permute-done.7), kind=kOutput, calls=%fused_computation.2 | convolution fusion | flops 1098907648 | bytes 27852800 | tf_op jit(solution)/shard_map/tcgd,scd->cgts/dot_general | solution.py:51
  331.2 11.5 %fusion.13 = bf16[2,8,512,512]{2,3,1,0:T(8,128)(2,1)} fusion(f32[2,512,512,8]{2,1,3,0:T(8,128)} %fusion.107, f32[2,8,512]{2,1,0:T(8,128)S(1)} %bitcast.449, f32[2,8,512]{2,1,0:T(8,128)S(1)} %bitcast.457, pred[512,512]{0,1:T(8,128)(4,1)S(1)} %copy-done.11, bf16[512,2,8,128]{3,2,1,0:T(8,128)(2,1)} %bitcast.423, bf16[512,2,128]{2,0,1:T(8,128)(2,1)} %collective-permute-done.1), kind=kOutput, calls=%fused_computation.20 | convolution fusion | flops 1098907648 | bytes 27852800 | tf_op jit(solution)/shard_map/tcgd,scd->cgts/dot_general | solution.py:51
  342.7 8.8 %fusion.121 = f32[2,8,512,128]{3,2,1,0:T(8,128)} fusion(bf16[2,8,512,512]{2,3,1,0:T(8,128)(2,1)} %fusion.13, bf16[512,2,128]{2,0,1:T(8,128)(2,1)S(1)} %collective-permute-done), kind=kOutput, calls=%fused_computation.134 | convolution fusion | flops 1073741824 | bytes 12845056 | tf_op jit(solution)/shard_map/cgts,scd->tcgd/dot_general | solution.py:57
  354.9 4.3 fusion.74
  359.2 10.9 %fusion.68 = f32[512,2,128]{2,0,1:T(8,128)} fusion(f32[512,2,128]{2,0,1:T(8,128)} %collective-permute-done.13, f32[2,512,512,8]{2,1,3,0:T(8,128)} %fusion.107, f32[2,8,512]{2,1,0:T(8,128)S(1)} %bitcast.458, pred[512,512]{0,1:T(8,128)(4,1)S(1)} %copy-done.11, bf16[512,2,8,128]{3,2,1,0:T(8,128)(2,1)} %bitcast.424), kind=kOutput, calls=%fused_computation.76 | convolution fusion | flops 1090650112 | bytes 20217856 | tf_op jit(solution)/shard_map/cgts,tcgd->scd/dot_general | solution.py:55
  373.2 5.9 %convolution_bitcast_fusion.3 = f32[512,2,128]{2,0,1:T(8,128)S(1)} fusion(bf16[2,8,512,512]{2,3,1,0:T(8,128)(2,1)} %copy-done.4, bf16[512,2,8,128]{3,2,1,0:T(8,128)(2,1)S(1)} %bitcast.388), kind=kOutput, calls=%fused_computation.68 | convolution fusion | flops 1073741824 | bytes 11010048 | tf_op jit(solution)/shard_map/cgts,tcgd->scd/dot_general | solution.py:56
  380.6 4.8 collective-permute-done.10
  391.1 5.5 %collective-permute-done.11 = f32[512,2,128]{2,0,1:T(8,128)S(1)} collective-permute-done((f32[512,2,128]{2,0,1:T(8,128)S(1)}, f32[512,2,128]{2,0,1:T(8,128)S(1)}, u32[]{:S(2)}, u32[]{:S(2)}) %collective-permute-start.11) | collective-permute-done | bytes 524320 | tf_op jit(solution)/shard_map/ppermute | solution.py:22
  400.1 7.8 %collective-permute-done.12 = bf16[512,2,128]{2,0,1:T(8,128)(2,1)S(1)} collective-permute-done((bf16[512,2,128]{2,0,1:T(8,128)(2,1)S(1)}, bf16[512,2,128]{2,0,1:T(8,128)(2,1)S(1)}, u32[]{:S(2)}, u32[]{:S(2)}) %collective-permute-start.12) | collective-permute-done | bytes 262176 | tf_op jit(solution)/shard_map/ppermute | solution.py:22
  423.2 5.0 all-to-all-start.8
  428.2 12.3 %fusion.41 = bf16[512,2,8,128]{3,0,2,1:T(8,128)(2,1)} fusion(f32[256,2,8,128]{3,0,2,1:T(8,128)S(1)} %convolution_bitcast_fusion.1, f32[256,2,8,128]{3,0,2,1:T(8,128)} %convolution_bitcast_fusion, f32[2,8,512,128]{3,2,1,0:T(8,128)} %fusion.113, f32[2,8,512,128]{3,2,1,0:T(8,128)} %fusion.117, f32[2,8,512,128]{3,2,1,0:T(8,128)} %fusion.121, ...), kind=kOutput, calls=%fused_computation.48 | convolution fusion | flops 1081081856 | bytes 27525120 | tf_op jit(solution)/shard_map/cgts,scd->tcgd/dot_general | solution.py:57
  445.7 5.1 %all-to-all-start.6 = ((bf16[4,128,2048]{2,1,0:T(8,128)(2,1)}), bf16[4,128,2048]{2,1,0:T(8,128)(2,1)S(1)}, u32[]{:S(2)}, u32[]{:S(2)}) async-start(bf16[4,128,2048]{2,1,0:T(8,128)(2,1)} %all_to_all.125), calls=%async_computation.6 | async-start | bytes 4194304 | tf_op jit(solution)/shard_map/all_to_all | solution.py:177
  452.9 44.6 %all-to-all-done.6 = bf16[4,128,2048]{2,1,0:T(8,128)(2,1)S(1)} async-done(((bf16[4,128,2048]{2,1,0:T(8,128)(2,1)}), bf16[4,128,2048]{2,1,0:T(8,128)(2,1)S(1)}, u32[]{:S(2)}, u32[]{:S(2)}) %all-to-all-start.6) | async-done | bytes 2097184 | tf_op jit(solution)/shard_map/all_to_all | solution.py:177
  (196 shorter events, 142.9 us)
Async XLA Ops:
  0.6 12.0 %all-to-all-start.2 = ((f32[128,4,16]{0,2,1:T(8,128)}), f32[128,4,16]{0,2,1:T(8,128)S(1)}, u32[]{:S(2)}, u32[]{:S(2)}) async-start(f32[128,4,16]{0,2,1:T(8,128)} %bitcast.459), calls=%async_computation.2 | async-start | bytes 65536 | tf_op jit(solution)/shard_map/all_to_all | solution.py:72
  12.6 11.3 %all-to-all-start = ((bf16[128,4,256]{2,0,1:T(8,128)(2,1)}), bf16[128,4,256]{2,0,1:T(8,128)(2,1)S(1)}, u32[]{:S(2)}, u32[]{:S(2)}) async-start(bf16[128,4,256]{2,0,1:T(8,128)(2,1)} %bitcast.376), calls=%async_computation | async-start | bytes 524288 | tf_op jit(solution)/shard_map/all_to_all | solution.py:85
  23.9 10.2 %all-to-all-start.3 = ((bf16[128,4,256]{2,0,1:T(8,128)(2,1)}), bf16[128,4,256]{2,0,1:T(8,128)(2,1)S(1)}, u32[]{:S(2)}, u32[]{:S(2)}) async-start(bf16[128,4,256]{2,0,1:T(8,128)(2,1)} %bitcast.375), calls=%async_computation.3 | async-start | bytes 524288 | tf_op jit(solution)/shard_map/all_to_all | solution.py:86
  34.1 48.5 %all-to-all-start.1 = ((bf16[128,4,2048]{2,0,1:T(8,128)(2,1)}), bf16[128,4,2048]{2,0,1:T(8,128)(2,1)S(1)}, u32[]{:S(2)}, u32[]{:S(2)}) async-start(bf16[128,4,2048]{2,0,1:T(8,128)(2,1)} %bitcast.403), calls=%async_computation.1 | async-start | bytes 4194304 | tf_op jit(solution)/shard_map/all_to_all | solution.py:68
  83.9 51.3 %all-to-all-start.4 = ((bf16[128,4,2048]{2,0,1:T(8,128)(2,1)}), bf16[128,4,2048]{2,0,1:T(8,128)(2,1)S(1)}, u32[]{:S(2)}, u32[]{:S(2)}) async-start(bf16[128,4,2048]{2,0,1:T(8,128)(2,1)} %bitcast.401), calls=%async_computation.4 | async-start | bytes 4194304 | tf_op jit(solution)/shard_map/all_to_all | solution.py:70
  87.6 52.0 %copy-start.23 = (s32[3]{0:T(128)S(1)}, s32[3]{0:T(128)}, u32[]{:S(2)}) copy-start(s32[3]{0:T(128)} %param.14) | copy-start | bytes 40
  135.2 32.9 %copy-start = (bf16[128,4,2048]{2,0,1:T(8,128)(2,1)}, bf16[128,4,2048]{2,0,1:T(8,128)(2,1)S(1)}, u32[]{:S(2)}) copy-start(bf16[128,4,2048]{2,0,1:T(8,128)(2,1)S(1)} %all-to-all-done.4) | copy-start | bytes 6291460
  135.2 52.2 %all-to-all-start.5 = ((bf16[128,4,2048]{2,0,1:T(8,128)(2,1)}), bf16[128,4,2048]{2,0,1:T(8,128)(2,1)}, u32[]{:S(2)}, u32[]{:S(2)}) async-start(bf16[128,4,2048]{2,0,1:T(8,128)(2,1)} %bitcast.400), calls=%async_computation.5 | async-start | bytes 4194304 | tf_op jit(solution)/shard_map/all_to_all | solution.py:69
  141.5 5.7 %collective-permute-start.1 = (bf16[512,2,128]{2,0,1:T(8,128)(2,1)}, bf16[512,2,128]{2,0,1:T(8,128)(2,1)}, u32[]{:S(2)}, u32[]{:S(2)}) collective-permute-start(bf16[512,2,128]{2,0,1:T(8,128)(2,1)} %copy.249), channel_id=1, source_target_pairs={{0,4},{4,8},{8,12},{12,16},{16,20},{20,24},{24,28},{1,5},{5,9},{9,... | collective-permute-start | bytes 786440 | tf_op jit(solution)/shard_map/ppermute | solution.py:17
  143.5 7.7 %collective-permute-start = (bf16[512,2,128]{2,0,1:T(8,128)(2,1)S(1)}, bf16[512,2,128]{2,0,1:T(8,128)(2,1)S(1)}, u32[]{:S(2)}, u32[]{:S(2)}) collective-permute-start(bf16[512,2,128]{2,0,1:T(8,128)(2,1)S(1)} %copy.247), channel_id=1, source_target_pairs={{0,4},{4,8},{8,12},{12,16},{16,20},{20,24},{24,28},{1,5},{5,9},{9,... | collective-permute-start | bytes 786440 | tf_op jit(solution)/shard_map/ppermute | solution.py:17
  147.1 8.0 %collective-permute-start.3 = (bf16[512,2,128]{2,0,1:T(8,128)(2,1)}, bf16[512,2,128]{2,0,1:T(8,128)(2,1)}, u32[]{:S(2)}, u32[]{:S(2)}) collective-permute-start(bf16[512,2,128]{2,0,1:T(8,128)(2,1)} %collective-permute-done.1), channel_id=1, source_target_pairs={{0,4},{4,8},{8,12},{12,16},{16,20},{20,24},{24,28},{1,5},{5,9},{9,... | collective-permute-start | bytes 786440 | tf_op jit(solution)/shard_map/ppermute | solution.py:17
  151.2 8.0 %collective-permute-start.2 = (bf16[512,2,128]{2,0,1:T(8,128)(2,1)S(1)}, bf16[512,2,128]{2,0,1:T(8,128)(2,1)S(1)}, u32[]{:S(2)}, u32[]{:S(2)}) collective-permute-start(bf16[512,2,128]{2,0,1:T(8,128)(2,1)S(1)} %collective-permute-done), channel_id=1, source_target_pairs={{0,4},{4,8},{8,12},{12,16},{16,20},{20,24},{24,28},{1,5},{5,9},{9,... | collective-permute-start | bytes 786440 | tf_op jit(solution)/shard_map/ppermute | solution.py:17
  155.1 13.2 %collective-permute-start.5 = (bf16[512,2,128]{2,0,1:T(8,128)(2,1)}, bf16[512,2,128]{2,0,1:T(8,128)(2,1)}, u32[]{:S(2)}, u32[]{:S(2)}) collective-permute-start(bf16[512,2,128]{2,0,1:T(8,128)(2,1)} %collective-permute-done.3), channel_id=1, source_target_pairs={{0,4},{4,8},{8,12},{12,16},{16,20},{20,24},{24,28},{1,5},{5,9},{9,... | collective-permute-start | bytes 786440 | tf_op jit(solution)/shard_map/ppermute | solution.py:17
  159.2 11.9 %collective-permute-start.4 = (bf16[512,2,128]{2,0,1:T(8,128)(2,1)S(1)}, bf16[512,2,128]{2,0,1:T(8,128)(2,1)}, u32[]{:S(2)}, u32[]{:S(2)}) collective-permute-start(bf16[512,2,128]{2,0,1:T(8,128)(2,1)S(1)} %collective-permute-done.2), channel_id=1, source_target_pairs={{0,4},{4,8},{8,12},{12,16},{16,20},{20,24},{24,28},{1,5},{5,9},{9,... | collective-permute-start | bytes 786440 | tf_op jit(solution)/shard_map/ppermute | solution.py:17
  168.3 151.5 %collective-permute-start.7 = (bf16[512,2,128]{2,0,1:T(8,128)(2,1)}, bf16[512,2,128]{2,0,1:T(8,128)(2,1)}, u32[]{:S(2)}, u32[]{:S(2)}) collective-permute-start(bf16[512,2,128]{2,0,1:T(8,128)(2,1)} %collective-permute-done.5), channel_id=1, source_target_pairs={{0,4},{4,8},{8,12},{12,16},{16,20},{20,24},{24,28},{1,5},{5,9},{9,... | collective-permute-start | bytes 786440 | tf_op jit(solution)/shard_map/ppermute | solution.py:17
  171.1 82.3 %collective-permute-start.6 = (bf16[512,2,128]{2,0,1:T(8,128)(2,1)}, bf16[512,2,128]{2,0,1:T(8,128)(2,1)S(1)}, u32[]{:S(2)}, u32[]{:S(2)}) collective-permute-start(bf16[512,2,128]{2,0,1:T(8,128)(2,1)} %collective-permute-done.4), channel_id=1, source_target_pairs={{0,4},{4,8},{8,12},{12,16},{16,20},{20,24},{24,28},{1,5},{5,9},{9,... | collective-permute-start | bytes 786440 | tf_op jit(solution)/shard_map/ppermute | solution.py:17
  198.4 84.9 %copy-start.16 = (f32[512,16]{0,1:T(8,128)}, f32[512,16]{0,1:T(8,128)S(1)}, u32[]{:S(2)}) copy-start(f32[512,16]{0,1:T(8,128)S(1)} %copy.237) | copy-start | bytes 98308
  215.0 138.9 %collective-permute-start.8 = (f32[512,2,128]{2,0,1:T(8,128)}, f32[512,2,128]{2,0,1:T(8,128)}, u32[]{:S(2)}, u32[]{:S(2)}) collective-permute-start(f32[512,2,128]{2,0,1:T(8,128)} %fusion.75), channel_id=1, source_target_pairs={{0,4},{4,8},{8,12},{12,16},{16,20},{20,24},{24,28},{28,0},{1,5},{5... | collective-permute-start | bytes 1572872 | tf_op jit(solution)/shard_map/ppermute | solution.py:22
  215.0 144.2 %collective-permute-start.13 = (f32[512,2,128]{2,0,1:T(8,128)}, f32[512,2,128]{2,0,1:T(8,128)}, u32[]{:S(2)}, u32[]{:S(2)}) collective-permute-start(f32[512,2,128]{2,0,1:T(8,128)} %fusion.71), channel_id=1, source_target_pairs={{0,4},{4,8},{8,12},{12,16},{16,20},{20,24},{24,28},{28,0},{1,5},{5... | collective-permute-start | bytes 1572872 | tf_op jit(solution)/shard_map/ppermute | solution.py:22
  319.8 31.7 %slice-start.2 = ((s8[8388608]{0:T(1024)(128)(4,1)}), s8[4194304]{0:T(1024)(128)(4,1)S(1)}, s32[]{:S(2)}) async-start(s8[8388608]{0:T(1024)(128)(4,1)} %bitcast.398), calls=%async_computation.11 | async-start | bytes 8388608
  331.2 20.3 %slice-start.3 = ((s8[8388608]{0:T(1024)(128)(4,1)}), s8[4194304]{0:T(1024)(128)(4,1)S(1)}, s32[]{:S(2)}) async-start(s8[8388608]{0:T(1024)(128)(4,1)} %bitcast.398), calls=%async_computation.12 | async-start | bytes 8388608
  359.2 12.5 %collective-permute-start.9 = (f32[512,2,128]{2,0,1:T(8,128)}, f32[512,2,128]{2,0,1:T(8,128)}, u32[]{:S(2)}, u32[]{:S(2)}) collective-permute-start(f32[512,2,128]{2,0,1:T(8,128)} %fusion.74), channel_id=1, source_target_pairs={{0,4},{4,8},{8,12},{12,16},{16,20},{20,24},{24,28},{28,0},{1,5},{5... | collective-permute-start | bytes 1572872 | tf_op jit(solution)/shard_map/ppermute | solution.py:22
  370.1 9.7 %collective-permute-start.14 = (f32[512,2,128]{2,0,1:T(8,128)}, f32[512,2,128]{2,0,1:T(8,128)S(1)}, u32[]{:S(2)}, u32[]{:S(2)}) collective-permute-start(f32[512,2,128]{2,0,1:T(8,128)} %fusion.68), channel_id=1, source_target_pairs={{0,4},{4,8},{8,12},{12,16},{16,20},{20,24},{24,28},{28,0},{1,5},{5... | collective-permute-start | bytes 1572872 | tf_op jit(solution)/shard_map/ppermute | solution.py:22
  372.9 12.5 %collective-permute-start.10 = (f32[512,2,128]{2,0,1:T(8,128)S(1)}, f32[512,2,128]{2,0,1:T(8,128)S(1)}, u32[]{:S(2)}, u32[]{:S(2)}) collective-permute-start(f32[512,2,128]{2,0,1:T(8,128)S(1)} %add.246), channel_id=1, source_target_pairs={{0,4},{4,8},{8,12},{12,16},{16,20},{20,24},{24,28},{28,0},{1,5},{5... | collective-permute-start | bytes 1572872 | tf_op jit(solution)/shard_map/ppermute | solution.py:22
  379.8 11.2 %collective-permute-start.15 = (f32[512,2,128]{2,0,1:T(8,128)S(1)}, f32[512,2,128]{2,0,1:T(8,128)S(1)}, u32[]{:S(2)}, u32[]{:S(2)}) collective-permute-start(f32[512,2,128]{2,0,1:T(8,128)S(1)} %add.251), channel_id=1, source_target_pairs={{0,4},{4,8},{8,12},{12,16},{16,20},{20,24},{24,28},{28,0},{1,5},{5... | collective-permute-start | bytes 1572872 | tf_op jit(solution)/shard_map/ppermute | solution.py:22
  385.4 11.2 %collective-permute-start.11 = (f32[512,2,128]{2,0,1:T(8,128)S(1)}, f32[512,2,128]{2,0,1:T(8,128)S(1)}, u32[]{:S(2)}, u32[]{:S(2)}) collective-permute-start(f32[512,2,128]{2,0,1:T(8,128)S(1)} %add.247), channel_id=1, source_target_pairs={{0,4},{4,8},{8,12},{12,16},{16,20},{20,24},{24,28},{28,0},{1,5},{5... | collective-permute-start | bytes 1572872 | tf_op jit(solution)/shard_map/ppermute | solution.py:22
  391.1 21.4 %collective-permute-start.16 = (f32[512,2,128]{2,0,1:T(8,128)S(1)}, f32[512,2,128]{2,0,1:T(8,128)}, u32[]{:S(2)}, u32[]{:S(2)}) collective-permute-start(f32[512,2,128]{2,0,1:T(8,128)S(1)} %add.252), channel_id=1, source_target_pairs={{0,4},{4,8},{8,12},{12,16},{16,20},{20,24},{24,28},{28,0},{1,5},{5... | collective-permute-start | bytes 1572872 | tf_op jit(solution)/shard_map/ppermute | solution.py:22
  396.7 11.2 %collective-permute-start.12 = (bf16[512,2,128]{2,0,1:T(8,128)(2,1)S(1)}, bf16[512,2,128]{2,0,1:T(8,128)(2,1)S(1)}, u32[]{:S(2)}, u32[]{:S(2)}) collective-permute-start(bf16[512,2,128]{2,0,1:T(8,128)(2,1)S(1)} %add_convert_fusion.1), channel_id=1, source_target_pairs={{0,16},{4,20},{8,24},{12,28},{16,0},{20,4},{24,8},{28,12},{1,17},{... | collective-permute-start | bytes 786440 | tf_op jit(solution)/shard_map/ppermute | solution.py:22
  409.1 14.1 %all-to-all-start.7 = ((bf16[4,128,256]{2,1,0:T(8,128)(2,1)}), bf16[4,128,256]{2,1,0:T(8,128)(2,1)S(1)}, u32[]{:S(2)}, u32[]{:S(2)}) async-start(bf16[4,128,256]{2,1,0:T(8,128)(2,1)} %convert_element_type.114), calls=%async_computation.7 | async-start | bytes 524288 | tf_op jit(solution)/shard_map/all_to_all | solution.py:163
  413.7 8.3 %collective-permute-start.17 = (bf16[512,2,128]{2,0,1:T(8,128)(2,1)S(1)}, bf16[512,2,128]{2,0,1:T(8,128)(2,1)S(1)}, u32[]{:S(2)}, u32[]{:S(2)}) collective-permute-start(bf16[512,2,128]{2,0,1:T(8,128)(2,1)S(1)} %add_convert_fusion), channel_id=1, source_target_pairs={{0,16},{4,20},{8,24},{12,28},{16,0},{20,4},{24,8},{28,12},{1,17},{... | collective-permute-start | bytes 786440 | tf_op jit(solution)/shard_map/ppermute | solution.py:22
  423.2 22.6 %all-to-all-start.8 = ((bf16[4,128,256]{2,1,0:T(8,128)(2,1)}), bf16[4,128,256]{2,1,0:T(8,128)(2,1)S(1)}, u32[]{:S(2)}, u32[]{:S(2)}) async-start(bf16[4,128,256]{2,1,0:T(8,128)(2,1)} %convert_element_type.122), calls=%async_computation.8 | async-start | bytes 524288 | tf_op jit(solution)/shard_map/all_to_all | solution.py:166
  445.7 51.7 %all-to-all-start.6 = ((bf16[4,128,2048]{2,1,0:T(8,128)(2,1)}), bf16[4,128,2048]{2,1,0:T(8,128)(2,1)S(1)}, u32[]{:S(2)}, u32[]{:S(2)}) async-start(bf16[4,128,2048]{2,1,0:T(8,128)(2,1)} %all_to_all.125), calls=%async_computation.6 | async-start | bytes 4194304 | tf_op jit(solution)/shard_map/all_to_all | solution.py:177
  (23 other events, 147.7 us)
where the time goes:
time: 509 us; the launch traced here: 504 us
  matrix products  192 us (38%)
  waiting for transfers between devices  176 us (35%)
  starting transfers between devices  74.8 us (15%)
  local copies, waits for them, and re-layouts  46.5 us (9%)
  other arithmetic  13.2 us (3%)
    dot_general x6, matrix products, piece_grads(): jnp.einsum('tcgd,scd->cgts', g_group, values, preferred_element_type=f32)  48.8 us
    dot_general x6, matrix products, piece_grads(): jnp.einsum('cgts,scd->tcgd', dscores_b, keys, preferred_element_type=f32)  44.9 us
    dot_general x6, matrix products, piece_grads(): jnp.einsum('cgts,tcgd->scd', probs_b, g_group, preferred_element_type=f32)  44.8 us
    all_to_all x1, waiting for transfers between devices, shards(): lax.all_to_all(dq_rows, 'head', split_axis=0, concat_axis=1, tiled=True)  44.6 us
    all_to_all x1, waiting for transfers between devices, shards(): lax.all_to_all(out_grad, 'head', split_axis=1, concat_axis=0, tiled=True)  43.7 us
    all_to_all x1, waiting for transfers between devices, shards(): lax.all_to_all(query, 'head', split_axis=1, concat_axis=0, tiled=True)  41.8 us
    dot_general x6, matrix products, piece_grads(): jnp.einsum('tcgd,scd->cgts', q_group, keys, preferred_element_type=f32)  35.5 us
    ppermute x8, starting transfers between devices, from_behind(): return lax.ppermute(value, axis, pairs)  28.9 us
  transfers between devices with their start and end apart: 27, of which 13 were waited for; matrix products, arithmetic and copies ran while one was open for 48% of the time, Pallas kernels for 0%

commit v1 on v0

v1 whole, which is shorter than its diff:
```python
import functools
import math

import jax
import jax.numpy as jnp
from jax import lax
from jax.experimental import pallas as pl
from jax.experimental.pallas import tpu as pltpu
from jax.sharding import PartitionSpec as P

KVH = 8
HD = 128
DOC_MAX = 2048
BLOCK = 128
LOG2E = 1.4426950408889634
FAR = 1 << 20


def attention_kernel(
    range_rows, info, starts, keep, qg_ref, stats_ref, kv_ref, dq_ref, dkv_ref,
    k_all, v_all, kt_all, dk_acc, dv_acc, dqt_acc, blocks,
):
    f32 = jnp.float32
    step = pl.program_id(0)
    steps = pl.num_programs(0)
    parts, ranges, _, rows, _ = kv_ref.shape
    group = qg_ref.shape[3] // HD
    total = group * rows
    width = min(total, 256)
    scale = 1.0 / math.sqrt(HD)
    offset = info[0]

    @pl.when(step == 0)
    def _():
        for t in range(ranges):
            for z in range(parts):
                first = (t * parts + z) * rows
                k_all[first : first + rows, :] = kv_ref[z, t, 0]
                v_all[first : first + rows, :] = kv_ref[z, t, 1]
        for first in range(0, k_all.shape[0], 256):
            piece = k_all[first : first + 256, :].astype(f32)
            kt_all[:, first : first + 256] = piece.T.astype(jnp.bfloat16)
        dk_acc[...] = jnp.zeros_like(dk_acc)
        dv_acc[...] = jnp.zeros_like(dv_acc)

    first_query = step * range_rows + offset
    query_block = first_query // BLOCK

    def doc_start(position):
        found = jnp.zeros_like(position)
        for d in range(starts.shape[0]):
            found = jnp.maximum(found, jnp.where(starts[d] <= position, starts[d], 0))
        return found

    first_start = doc_start(first_query)

    def list_block(j, count):
        kept = keep[query_block, query_block - j] == 1
        reaches = (j + 1) * BLOCK > first_start
        blocks[count] = j
        return count + jnp.where(kept & reaches, 1, 0)

    count = lax.fori_loop(0, query_block + 1, list_block, jnp.int32(0))
    blocks[count] = -1

    dqt_acc[...] = jnp.zeros_like(dqt_acc)
    row_query = first_query + lax.broadcasted_iota(jnp.int32, (1, width), 1) % rows
    row_start = doc_start(row_query)
    queries = [qg_ref[0, 0, :, h * HD : (h + 1) * HD] for h in range(group)]
    grads = [qg_ref[0, 1, :, h * HD : (h + 1) * HD] for h in range(group)]
    queries = jnp.concatenate(queries, axis=0)
    grads = jnp.concatenate(grads, axis=0)

    def pair(p, _):
        j0 = blocks[2 * p]
        j1 = blocks[2 * p + 1]
        j1_first = jnp.where(j1 < 0, FAR, j1 * BLOCK)
        at0 = pl.ds(pl.multiple_of(j0 * BLOCK, BLOCK), BLOCK)
        at1 = pl.ds(pl.multiple_of(jnp.maximum(j1, 0) * BLOCK, BLOCK), BLOCK)
        keys = jnp.concatenate([k_all[at0, :], k_all[at1, :]], axis=0)
        values = jnp.concatenate([v_all[at0, :], v_all[at1, :]], axis=0)
        keys_t = jnp.concatenate([kt_all[:, at0], kt_all[:, at1]], axis=1)
        line = lax.broadcasted_iota(jnp.int32, (2 * BLOCK, width), 0)
        key_pos = jnp.where(line < BLOCK, line + j0 * BLOCK, line - BLOCK + j1_first)
        allowed = (key_pos <= row_query) & (key_pos >= row_start)
        probs_all, dscores_all = [], []
        for first in range(0, total, width):
            q = queries[first : first + width]
            g = grads[first : first + width]
            nt = (((1,), (1,)), ((), ()))
            s = lax.dot_general(keys, q, nt, preferred_element_type=f32)
            dp = lax.dot_general(values, g, nt, preferred_element_type=f32)
            lse = stats_ref[0, 0:1, first : first + width]
            delta = stats_ref[0, 1:2, first : first + width]
            probs = jnp.where(allowed, jnp.exp2(s * (scale * LOG2E) - lse), 0.0)
            dscores = probs * (dp - delta)
            probs_all.append(probs.astype(jnp.bfloat16))
            dscores_all.append(dscores.astype(jnp.bfloat16))
        probs_all = jnp.concatenate(probs_all, axis=1)
        dscores_all = jnp.concatenate(dscores_all, axis=1)
        dv = jnp.dot(probs_all, grads, preferred_element_type=f32)
        dk = jnp.dot(dscores_all, queries, preferred_element_type=f32)
        dqt_acc[...] += jnp.dot(keys_t, dscores_all, preferred_element_type=f32)
        dv_acc[at0, :] += dv[:BLOCK]
        dk_acc[at0, :] += dk[:BLOCK]
        dv_acc[at1, :] += dv[BLOCK:]
        dk_acc[at1, :] += dk[BLOCK:]
        return 0

    lax.fori_loop(0, (count + 1) // 2, pair, 0)
    for first in range(0, total, width):
        dq = (dqt_acc[:, first : first + width] * scale).T.astype(jnp.bfloat16)
        for h in range(width // rows):
            head = first // rows + h
            dq_ref[0, :, head * HD : (head + 1) * HD] = dq[h * rows : (h + 1) * rows]

    @pl.when(step == steps - 1)
    def _():
        for t in range(ranges):
            for z in range(parts):
                first = (t * parts + z) * rows
                dkv_ref[z, t, 0] = (dk_acc[first : first + rows, :] * scale).astype(jnp.bfloat16)
                dkv_ref[z, t, 1] = dv_acc[first : first + rows, :].astype(jnp.bfloat16)


def attention(info, starts, keep, qg, stats, kv, range_rows):
    ranges, _, rows, columns = qg.shape
    parts = kv.shape[0]
    span = parts * ranges * rows
    total = rows * columns // HD
    smem = pl.BlockSpec(memory_space=pltpu.SMEM)
    f32, bf16 = jnp.float32, jnp.bfloat16
    return pl.pallas_call(
        functools.partial(attention_kernel, range_rows),
        grid=(ranges,),
        out_shape=(
            jax.ShapeDtypeStruct((ranges, rows, columns), bf16),
            jax.ShapeDtypeStruct(kv.shape, bf16),
        ),
        in_specs=[
            smem, smem, smem,
            pl.BlockSpec((1, 2, rows, columns), lambda t: (t, 0, 0, 0)),
            pl.BlockSpec((1, 2, total), lambda t: (t, 0, 0)),
            pl.BlockSpec(kv.shape, lambda t: (0, 0, 0, 0, 0)),
        ],
        out_specs=(
            pl.BlockSpec((1, rows, columns), lambda t: (t, 0, 0)),
            pl.BlockSpec(kv.shape, lambda t: (0, 0, 0, 0, 0)),
        ),
        scratch_shapes=[
            pltpu.VMEM((span, HD), bf16),
            pltpu.VMEM((span, HD), bf16),
            pltpu.VMEM((HD, span), bf16),
            pltpu.VMEM((span, HD), f32),
            pltpu.VMEM((span, HD), f32),
            pltpu.VMEM((HD, total), f32),
            pltpu.SMEM((64,), jnp.int32),
        ],
        compiler_params=pltpu.CompilerParams(vmem_limit_bytes=40 * 1024 * 1024),
        cost_estimate=pl.CostEstimate(
            flops=5 * 2 * total * span * HD * ranges // 2,
            bytes_accessed=3 * ranges * rows * columns * 2 + 4 * span * HD * 2,
            transcendentals=total * span * ranges // 2,
        ),
    )(info, starts, keep, qg, stats, kv)


def shards(query, key, value, output, out_grad, lse, doc_lengths, block_keep):
    f32, bf16 = jnp.float32, jnp.bfloat16
    rows = query.shape[0]
    parts = lax.axis_size("head")
    range_rows = rows * parts
    ranges = DOC_MAX // range_rows
    blks = lax.axis_size("blk")
    groups = [[w + r for r in range(ranges)] for w in range(0, blks, ranges)]
    chunks = KVH // ranges
    heads = query.shape[1] // HD
    group = heads // KVH
    columns = group * HD
    sub = lax.axis_index("head")
    window = lax.axis_index("blk") // ranges

    def swap(array):
        return lax.all_to_all(array, "blk", 0, 0, axis_index_groups=groups)

    starts = (jnp.cumsum(doc_lengths) - doc_lengths - window * DOC_MAX).astype(jnp.int32)
    info = jnp.full((1,), sub * rows, jnp.int32)
    keep = lax.all_gather(block_keep, "blk", axis_index_groups=groups, tiled=True)

    q5 = query.reshape(rows, ranges, chunks, columns)
    g5 = out_grad.reshape(rows, ranges, chunks, columns)
    k5 = key.reshape(rows, ranges, chunks, HD)
    v5 = value.reshape(rows, ranges, chunks, HD)
    kv_in, qg_in = [], []
    for c in range(chunks):
        kv = jnp.stack([k5[:, :, c], v5[:, :, c]], axis=0).transpose(2, 0, 1, 3)
        kv_in.append(lax.all_gather(swap(kv), "head"))
        qg = jnp.stack([q5[:, :, c], g5[:, :, c]], axis=0).transpose(2, 0, 1, 3)
        qg_in.append(swap(qg))
    delta = jnp.sum(
        out_grad.reshape(rows, heads, HD).astype(f32) * output.reshape(rows, heads, HD).astype(f32),
        axis=2,
    )
    stats = jnp.stack([lse * LOG2E, delta], axis=0)
    stats = stats.reshape(2, rows, ranges, chunks, group).transpose(2, 3, 0, 4, 1)
    stats = swap(stats.reshape(ranges, chunks, 2, group * rows))

    dq_out, dkv_out = [], []
    for c in range(chunks):
        dq, dkv = attention(info, starts, keep, qg_in[c], stats[:, c], kv_in[c], range_rows)
        dq_out.append(swap(dq))
        partial = lax.all_to_all(dkv, "head", 0, 0)
        summed = jnp.sum(partial.astype(f32), axis=0).astype(bf16)
        dkv_out.append(swap(summed))
    query_grad = jnp.stack(dq_out, axis=1).transpose(2, 0, 1, 3).reshape(rows, heads * HD)
    dkv = jnp.stack(dkv_out, axis=1)
    key_grad = dkv[:, :, 0].transpose(2, 0, 1, 3).reshape(rows, KVH * HD)
    value_grad = dkv[:, :, 1].transpose(2, 0, 1, 3).reshape(rows, KVH * HD)
    return (query_grad, key_grad, value_grad)


def solution(mesh):
    tokens = P(("blk", "head"), None)
    in_specs = (tokens, tokens, tokens, tokens, tokens, tokens, P(), P("blk", None))
    out_specs = (tokens, tokens, tokens)
    return jax.shard_map(shards, mesh=mesh, in_specs=in_specs, out_specs=out_specs, check_vma=False)
```

time: 509 us -> 259 us (0.51)
  the two profiles are of different devices: /device:TPU:0 before, /device:TPU:7 now
where the time goes in v1:
time: 259 us; the launch traced here: 256 us
  blocking collectives  74.3 us (29%)
  waiting for transfers between devices  44.6 us (17%)
  starting transfers between devices  43.4 us (17%)
  local copies, waits for them, and re-layouts  37.2 us (14%)
  Pallas kernels  26 us (10%)
  other arithmetic  16.1 us (6%)
  between operations  14.3 us (6%)
    all_to_all x8, starting transfers between devices, swap(): return lax.all_to_all(array, 'blk', 0, 0, axis_index_groups=groups)  39.9 us
    all_to_all x1, blocking collectives, shards(): partial = lax.all_to_all(dkv, 'head', 0, 0)  34.5 us
    pallas_call x2, Pallas kernels, attention(): pl.pallas_call(functools.partial(attention_kernel, range_rows), grid=(ran...  26 us
    unnamed x38, local copies, waits for them, and re-layouts  25.2 us
    all_to_all x1, waiting for transfers between devices, shards(): partial = lax.all_to_all(dkv, 'head', 0, 0)  24.3 us
    all_gather x1, blocking collectives, shards(): lax.all_gather(block_keep, 'blk', axis_index_groups=groups, tiled=True)  24.1 us
    all_to_all x8, waiting for transfers between devices, swap(): return lax.all_to_all(array, 'blk', 0, 0, axis_index_groups=groups)  20.3 us
    all_to_all x1, blocking collectives, swap(): return lax.all_to_all(array, 'blk', 0, 0, axis_index_groups=groups)  15.7 us
  transfers between devices with their start and end apart: 11, of which 4 were waited for; matrix products, arithmetic and copies ran while one was open for 14% of the time, Pallas kernels for 10%

profile of v1, /device:TPU:7, one launch (start us, length us, event | category | flops | bytes accessed | tf_op | source)
XLA Modules:
  0.0 256.0 jit_solution(608248563114967609)
XLA Ops:
  7.2 2.7 %multiply_bitcast_fusion = f32[16,8,64,128]{3,1,2,0:T(8,128)S(1)} fusion(bf16[128,8192]{1,0:T(8,128)(2,1)} %param.11, bf16[128,8192]{1,0:T(8,128)(2,1)} %param.12), kind=kLoop, calls=%fused_computation | loop fusion | flops 3145728 | bytes 8388608
  9.9 2.7 %copy.120 = f32[16,8,64,128]{3,2,1,0:T(8,128)} copy(f32[16,8,64,128]{3,1,2,0:T(8,128)S(1)} %multiply_bitcast_fusion) | data formatting | bytes 8388608
  12.6 3.4 %reduce_sum.33 = f32[128,64]{1,0:T(8,128)S(1)} reduce(f32[128,64,128]{2,1,0:T(8,128)} %bitcast.78, f32[]{:T(128)} %constant.37.clone.1), dimensions={2}, to_apply=%region_1.2 | reduce | flops 1040384 | bytes 4227076 | tf_op jit(solution)/shard_map/reduce_sum | solution.py:200
  16.9 4.1 %all-to-all-start.1 = ((f32[4,2,2,1024]{3,2,1,0:T(2,128)}), f32[4,2,2,1024]{3,2,1,0:T(2,128)S(1)}, u32[]{:S(2)}, u32[]{:S(2)}) async-start(f32[4,2,2,1024]{3,2,1,0:T(2,128)} %copy.93), calls=%async_computation.1 | async-start | bytes 131072 | tf_op jit(solution)/shard_map/all_to_all | solution.py:184
  21.5 2.4 copy.90
  23.9 3.2 %copy.88 = bf16[128,8192]{0,1:T(8,128)(2,1)S(1)} copy(bf16[128,8192]{1,0:T(8,128)(2,1)} %param.8) | data formatting | bytes 4194304 | tf_op args[0]
  28.6 3.4 %all-to-all-start.5 = ((bf16[4,2,128,128]{2,3,1,0:T(8,128)(2,1)}), bf16[4,2,128,128]{2,3,1,0:T(8,128)(2,1)S(1)}, u32[]{:S(2)}, u32[]{:S(2)}) async-start(bf16[4,2,128,128]{2,3,1,0:T(8,128)(2,1)} %copy.104), calls=%async_computation.5 | async-start | bytes 524288 | tf_op jit(solution)/shard_map/all_to_all | solution.py:184
  32.0 2.7 %fusion.5 = (bf16[128,4,1,1024]{0,3,2,1:T(8,128)(2,1)S(1)}, bf16[128,4,1,1024]{0,3,2,1:T(8,128)(2,1)}) fusion(bf16[128,4,2,1024]{0,3,2,1:T(8,128)(2,1)} %bitcast.80), kind=kLoop, calls=%fused_computation.23 | loop fusion | bytes 4194304 | tf_op jit(solution)/shard_map/slice | solution.py:198
  34.7 1.5 all-to-all-done.5
  36.8 5.3 %all-to-all-start.2 = ((bf16[4,2,128,128]{2,3,1,0:T(8,128)(2,1)}), bf16[4,2,128,128]{2,3,1,0:T(8,128)(2,1)S(1)}, u32[]{:S(2)}, u32[]{:S(2)}) async-start(bf16[4,2,128,128]{2,3,1,0:T(8,128)(2,1)} %copy.98), calls=%async_computation.2 | async-start | bytes 524288 | tf_op jit(solution)/shard_map/all_to_all | solution.py:184
  42.1 1.5 fusion.4
  43.6 1.6 copy.117
  46.5 2.7 %maximum_bitcast_fusion.1 = bf16[4,2,128,1024]{3,2,1,0:T(8,128)(2,1)} fusion(bf16[1,128,4,1024]{3,1,0,2:T(8,128)(2,1)S(1)} %bitcast.84, bf16[1,128,4,1024]{3,1,0,2:T(8,128)(2,1)} %bitcast.85), kind=kLoop, calls=%fused_computation.2 | loop fusion | flops 1048576 | bytes 4194304 | tf_op jit(solution)/shard_map/transpose | solution.py:198
  49.2 3.6 %all-to-all-start.4 = ((bf16[4,2,128,1024]{3,2,1,0:T(8,128)(2,1)}), bf16[4,2,128,1024]{3,2,1,0:T(8,128)(2,1)S(1)}, u32[]{:S(2)}, u32[]{:S(2)}) async-start(bf16[4,2,128,1024]{3,2,1,0:T(8,128)(2,1)} %maximum_bitcast_fusion.1), calls=%async_computation.4 | async-start | bytes 4194304 | tf_op jit(solution)/shard_map/all_to_all | solution.py:184
  52.9 1.8 copy.105
  56.0 2.4 copy.112
  58.4 2.7 %maximum_bitcast_fusion = bf16[4,2,128,1024]{3,2,1,0:T(8,128)(2,1)} fusion(bf16[1,128,4,1024]{3,1,0,2:T(8,128)(2,1)S(1)} %bitcast.83, bf16[1,128,4,1024]{3,1,0,2:T(8,128)(2,1)} %bitcast.86), kind=kLoop, calls=%fused_computation.1 | loop fusion | flops 1048576 | bytes 4194304 | tf_op jit(solution)/shard_map/transpose | solution.py:198
  61.1 15.6 %all-to-all-done.4.qg_ref = bf16[4,2,128,1024]{3,2,1,0:T(8,128)(2,1)S(1)} async-done(((bf16[4,2,128,1024]{3,2,1,0:T(8,128)(2,1)}), bf16[4,2,128,1024]{3,2,1,0:T(8,128)(2,1)S(1)}, u32[]{:S(2)}, u32[]{:S(2)}) %all-to-all-start.4) | async-done | bytes 2097184 | tf_op jit(solution)/shard_map/all_to_all | solution.py:184
  76.8 6.2 %all-to-all-start = ((bf16[4,2,128,1024]{3,2,1,0:T(8,128)(2,1)}), bf16[4,2,128,1024]{3,2,1,0:T(8,128)(2,1)}, u32[]{:S(2)}, u32[]{:S(2)}) async-start(bf16[4,2,128,1024]{3,2,1,0:T(8,128)(2,1)} %maximum_bitcast_fusion), calls=%async_computation | async-start | bytes 4194304 | tf_op jit(solution)/shard_map/all_to_all | solution.py:184
  84.1 24.1 %all-gather.2 = s32[4,4,17]{2,1,0:T(4,128)S(1)} all-gather(s32[1,4,17]{2,1,0:T(4,128)S(1)} %bitcast.94), channel_id=1, replica_groups={{0,4,8,12},{16,20,24,28},{1,5,9,13},{17,21,25,29},{2,6,10,14},{18,22,26..., dimensions={0}, use_global_device_ids=true | all-gather | bytes 1360 | tf_op jit(solution)/shard_map/all_gather | solution.py:188
  109.4 12.3 %shard_map.104 = (bf16[4,128,1024]{2,1,0:T(8,128)(2,1)S(1)}, bf16[4,4,2,128,128]{4,3,2,1,0:T(8,128)(2,1)S(1)}) custom-call(s32[1]{0:T(128)} %bitcast.info, s32[3]{0:T(128)S(1)} %fusion.3.starts, s32[16,17]{1,0:T(8,128)S(1)} %bitcast.74, bf16[4,2,128,1024]{3,2,1,0:T(8,128)(2,1)S(1)} %all-to-all-done.4.qg_ref, f32[4,2,1024]{2,1,0:T(2,128)S(1)} %get-tuple-element.37.stats_ref, ...), custom_call_target="tpu_custom_call" | custom-call | flops 5368709120 | bytes 5242880 | tf_op jit(solution)/shard_map/pallas_call | solution.py:133
  122.7 5.7 %all-to-all-start.6 = ((bf16[4,128,1024]{2,1,0:T(8,128)(2,1)}), bf16[4,128,1024]{2,1,0:T(8,128)(2,1)}, u32[]{:S(2)}, u32[]{:S(2)}) async-start(bf16[4,128,1024]{2,1,0:T(8,128)(2,1)} %copy-done), calls=%async_computation.6 | async-start | bytes 2097152 | tf_op jit(solution)/shard_map/all_to_all | solution.py:184
  129.7 13.7 %shard_map.103 = (bf16[4,128,1024]{2,1,0:T(8,128)(2,1)S(1)}, bf16[4,4,2,128,128]{4,3,2,1,0:T(8,128)(2,1)}) custom-call(s32[1]{0:T(128)} %bitcast.info, s32[3]{0:T(128)S(1)} %fusion.3.starts, s32[16,17]{1,0:T(8,128)S(1)} %bitcast.75, bf16[4,2,128,1024]{3,2,1,0:T(8,128)(2,1)} %all-to-all-done.qg_ref, f32[4,2,1024]{2,1,0:T(2,128)S(1)} %get-tuple-element.36.stats_ref, ...), custom_call_target="tpu_custom_call" | custom-call | flops 5368709120 | bytes 5242880 | tf_op jit(solution)/shard_map/pallas_call | solution.py:133
  143.4 15.7 %all_to_all.55 = bf16[4,128,1024]{2,1,0:T(8,128)(2,1)} all-to-all(bf16[4,128,1024]{2,1,0:T(8,128)(2,1)S(1)} %get-tuple-element.7), channel_id=1, replica_groups={{0,4,8,12},{16,20,24,28},{1,5,9,13},{17,21,25,29},{2,6,10,14},{18,22,26..., dimensions={0} | all-to-all | bytes 2097152 | tf_op jit(solution)/shard_map/all_to_all | solution.py:184
  159.1 34.5 %all_to_all.56 = bf16[4,4,2,128,128]{4,3,2,1,0:T(8,128)(2,1)S(1)} all-to-all(bf16[4,4,2,128,128]{4,3,2,1,0:T(8,128)(2,1)S(1)} %get-tuple-element.10), channel_id=1, replica_groups=mesh['blk'=8,'head'=4] {'head'}, dimensions={0} | all-to-all | bytes 2097152 | tf_op jit(solution)/shard_map/all_to_all | solution.py:212
  193.6 3.5 %all-to-all-start.7 = ((bf16[4,4,2,128,128]{4,3,2,1,0:T(8,128)(2,1)}), bf16[4,4,2,128,128]{4,3,2,1,0:T(8,128)(2,1)S(1)}, u32[]{:S(2)}, u32[]{:S(2)}) async-start(bf16[4,4,2,128,128]{4,3,2,1,0:T(8,128)(2,1)} %get-tuple-element.9), calls=%async_computation.7 | async-start | bytes 2097152 | tf_op jit(solution)/shard_map/all_to_all | solution.py:212
  198.1 24.3 %all-to-all-done.7 = bf16[4,4,2,128,128]{4,3,2,1,0:T(8,128)(2,1)S(1)} async-done(((bf16[4,4,2,128,128]{4,3,2,1,0:T(8,128)(2,1)}), bf16[4,4,2,128,128]{4,3,2,1,0:T(8,128)(2,1)S(1)}, u32[]{:S(2)}, u32[]{:S(2)}) %all-to-all-start.7) | async-done | bytes 1048608 | tf_op jit(solution)/shard_map/all_to_all | solution.py:212
  222.3 5.6 %all-to-all-start.10 = ((bf16[4,2,128,128]{3,2,1,0:T(8,128)(2,1)}), bf16[4,2,128,128]{3,2,1,0:T(8,128)(2,1)S(1)}, u32[]{:S(2)}, u32[]{:S(2)}) async-start(bf16[4,2,128,128]{3,2,1,0:T(8,128)(2,1)} %reduce_sum.35), calls=%async_computation.10 | async-start | bytes 524288 | tf_op jit(solution)/shard_map/all_to_all | solution.py:184
  228.8 3.2 %all-to-all-done.10 = bf16[4,2,128,128]{3,2,1,0:T(8,128)(2,1)S(1)} async-done(((bf16[4,2,128,128]{3,2,1,0:T(8,128)(2,1)}), bf16[4,2,128,128]{3,2,1,0:T(8,128)(2,1)S(1)}, u32[]{:S(2)}, u32[]{:S(2)}) %all-to-all-start.10) | async-done | bytes 262176 | tf_op jit(solution)/shard_map/all_to_all | solution.py:184
  232.1 5.9 %all-to-all-start.8 = ((bf16[4,2,128,128]{3,2,1,0:T(8,128)(2,1)}), bf16[4,2,128,128]{3,2,1,0:T(8,128)(2,1)}, u32[]{:S(2)}, u32[]{:S(2)}) async-start(bf16[4,2,128,128]{3,2,1,0:T(8,128)(2,1)} %reduce_sum.34), calls=%async_computation.8 | async-start | bytes 524288 | tf_op jit(solution)/shard_map/all_to_all | solution.py:184
  239.4 2.6 %copy.106 = bf16[128,4,2,1024]{0,3,2,1:T(8,128)(2,1)} copy(bf16[128,4,2,1024]{3,0,1,2:T(8,128)(2,1)S(1)} %maximum_bitcast_fusion.2) | data formatting | bytes 4194304 | tf_op jit(solution)/shard_map/transpose | solution.py:215
  242.0 4.1 %copy.109 = bf16[128,8192]{1,0:T(8,128)(2,1)} copy(bf16[128,8192]{0,1:T(8,128)(2,1)} %bitcast.81) | data formatting | bytes 4194304
  (63 shorter events, 16.9 us)
Async XLA Ops:
  12.6 3.5 %copy-start.10 = (f32[128,64]{0,1:T(8,128)S(1)}, f32[128,64]{0,1:T(8,128)}, u32[]{:S(2)}) copy-start(f32[128,64]{0,1:T(8,128)} %param.13) | copy-start | bytes 98308
  12.6 8.4 %copy-start.8 = (bf16[128,1024]{1,0:T(8,128)(2,1)S(1)}, bf16[128,1024]{1,0:T(8,128)(2,1)}, u32[]{:S(2)}) copy-start(bf16[128,1024]{1,0:T(8,128)(2,1)} %param.10) | copy-start | bytes 786436
  12.6 8.5 %copy-start.9 = (bf16[128,1024]{1,0:T(8,128)(2,1)S(1)}, bf16[128,1024]{1,0:T(8,128)(2,1)}, u32[]{:S(2)}) copy-start(bf16[128,1024]{1,0:T(8,128)(2,1)} %param.9) | copy-start | bytes 786436
  16.0 5.4 %copy-start.3 = (bf16[128,8192]{1,0:T(8,128)(2,1)S(1)}, bf16[128,8192]{1,0:T(8,128)(2,1)}, u32[]{:S(2)}) copy-start(bf16[128,8192]{1,0:T(8,128)(2,1)} %param.12) | copy-start | bytes 6291460
  16.9 11.7 %all-to-all-start.1 = ((f32[4,2,2,1024]{3,2,1,0:T(2,128)}), f32[4,2,2,1024]{3,2,1,0:T(2,128)S(1)}, u32[]{:S(2)}, u32[]{:S(2)}) async-start(f32[4,2,2,1024]{3,2,1,0:T(2,128)} %copy.93), calls=%async_computation.1 | async-start | bytes 131072 | tf_op jit(solution)/shard_map/all_to_all | solution.py:184
  28.6 7.6 %all-to-all-start.5 = ((bf16[4,2,128,128]{2,3,1,0:T(8,128)(2,1)}), bf16[4,2,128,128]{2,3,1,0:T(8,128)(2,1)S(1)}, u32[]{:S(2)}, u32[]{:S(2)}) async-start(bf16[4,2,128,128]{2,3,1,0:T(8,128)(2,1)} %copy.104), calls=%async_computation.5 | async-start | bytes 524288 | tf_op jit(solution)/shard_map/all_to_all | solution.py:184
  36.1 0.7 copy-start.7
  36.8 12.4 %all-to-all-start.2 = ((bf16[4,2,128,128]{2,3,1,0:T(8,128)(2,1)}), bf16[4,2,128,128]{2,3,1,0:T(8,128)(2,1)S(1)}, u32[]{:S(2)}, u32[]{:S(2)}) async-start(bf16[4,2,128,128]{2,3,1,0:T(8,128)(2,1)} %copy.98), calls=%async_computation.2 | async-start | bytes 524288 | tf_op jit(solution)/shard_map/all_to_all | solution.py:184
  43.6 1.6 copy-start.5
  49.2 27.5 %all-to-all-start.4 = ((bf16[4,2,128,1024]{3,2,1,0:T(8,128)(2,1)}), bf16[4,2,128,1024]{3,2,1,0:T(8,128)(2,1)S(1)}, u32[]{:S(2)}, u32[]{:S(2)}) async-start(bf16[4,2,128,1024]{3,2,1,0:T(8,128)(2,1)} %maximum_bitcast_fusion.1), calls=%async_computation.4 | async-start | bytes 4194304 | tf_op jit(solution)/shard_map/all_to_all | solution.py:184
  52.9 55.3 %all-gather.8.cloned.1.call-start = ((), (), s32[]{:S(2)}) async-start(), calls=%async_computation.12 | async-start | bytes 1310720 | tf_op jit(solution)/shard_map/all_gather | solution.py:197
  56.0 2.4 copy-start.6
  61.1 22.7 %copy-start.12 = (s32[3]{0:T(128)S(1)}, s32[3]{0:T(128)}, u32[]{:S(2)}) copy-start(s32[3]{0:T(128)} %param.14) | copy-start | bytes 40
  61.1 22.9 %copy-start.11 = (s32[4,17]{1,0:T(4,128)S(1)}, s32[4,17]{1,0:T(4,128)}, u32[]{:S(2)}) copy-start(s32[4,17]{1,0:T(4,128)} %param.15) | copy-start | bytes 820
  76.8 46.0 %all-to-all-start = ((bf16[4,2,128,1024]{3,2,1,0:T(8,128)(2,1)}), bf16[4,2,128,1024]{3,2,1,0:T(8,128)(2,1)}, u32[]{:S(2)}, u32[]{:S(2)}) async-start(bf16[4,2,128,1024]{3,2,1,0:T(8,128)(2,1)} %maximum_bitcast_fusion), calls=%async_computation | async-start | bytes 4194304 | tf_op jit(solution)/shard_map/all_to_all | solution.py:184
  83.0 45.5 %all-gather.6.cloned.1.call-start = ((), (), s32[]{:S(2)}) async-start(), calls=%async_computation.11 | async-start | bytes 1310720 | tf_op jit(solution)/shard_map/all_gather | solution.py:197
  108.2 1.2 copy-start.1
  121.7 1.0 copy-start
  122.7 20.7 %all-to-all-start.6 = ((bf16[4,128,1024]{2,1,0:T(8,128)(2,1)}), bf16[4,128,1024]{2,1,0:T(8,128)(2,1)}, u32[]{:S(2)}, u32[]{:S(2)}) async-start(bf16[4,128,1024]{2,1,0:T(8,128)(2,1)} %copy-done), calls=%async_computation.6 | async-start | bytes 2097152 | tf_op jit(solution)/shard_map/all_to_all | solution.py:184
  128.5 1.2 copy-start.2
  193.6 28.7 %all-to-all-start.7 = ((bf16[4,4,2,128,128]{4,3,2,1,0:T(8,128)(2,1)}), bf16[4,4,2,128,128]{4,3,2,1,0:T(8,128)(2,1)S(1)}, u32[]{:S(2)}, u32[]{:S(2)}) async-start(bf16[4,4,2,128,128]{4,3,2,1,0:T(8,128)(2,1)} %get-tuple-element.9), calls=%async_computation.7 | async-start | bytes 2097152 | tf_op jit(solution)/shard_map/all_to_all | solution.py:212
  197.2 40.8 %copy-start.4 = (bf16[4,128,1024]{2,1,0:T(8,128)(2,1)S(1)}, bf16[4,128,1024]{2,1,0:T(8,128)(2,1)}, u32[]{:S(2)}) copy-start(bf16[4,128,1024]{2,1,0:T(8,128)(2,1)} %all_to_all.55) | copy-start | bytes 3145732
  222.3 9.7 %all-to-all-start.10 = ((bf16[4,2,128,128]{3,2,1,0:T(8,128)(2,1)}), bf16[4,2,128,128]{3,2,1,0:T(8,128)(2,1)S(1)}, u32[]{:S(2)}, u32[]{:S(2)}) async-start(bf16[4,2,128,128]{3,2,1,0:T(8,128)(2,1)} %reduce_sum.35), calls=%async_computation.10 | async-start | bytes 524288 | tf_op jit(solution)/shard_map/all_to_all | solution.py:184
  232.1 14.0 %all-to-all-start.8 = ((bf16[4,2,128,128]{3,2,1,0:T(8,128)(2,1)}), bf16[4,2,128,128]{3,2,1,0:T(8,128)(2,1)}, u32[]{:S(2)}, u32[]{:S(2)}) async-start(bf16[4,2,128,128]{3,2,1,0:T(8,128)(2,1)} %reduce_sum.34), calls=%async_computation.8 | async-start | bytes 524288 | tf_op jit(solution)/shard_map/all_to_all | solution.py:184
Sparse Core Ops, SparseCore 0:
  55.8 28.6 all-gather.7
  86.7 27.9 all-gather.5

commit v2 on v1

--- a/solution.py
+++ b/solution.py
@@ -14,6 +14,7 @@
 BLOCK = 128
 LOG2E = 1.4426950408889634
 FAR = 1 << 20
+MESH = pl.DeviceIdType.MESH
 
 
 def attention_kernel(
@@ -21,8 +22,8 @@
     k_all, v_all, kt_all, dk_acc, dv_acc, dqt_acc, blocks,
 ):
     f32 = jnp.float32
-    step = pl.program_id(0)
-    steps = pl.num_programs(0)
+    step = pl.program_id(1)
+    steps = pl.num_programs(1)
     parts, ranges, _, rows, _ = kv_ref.shape
     group = qg_ref.shape[3] // HD
     total = group * rows
@@ -55,7 +56,7 @@
     first_start = doc_start(first_query)
 
     def list_block(j, count):
-        kept = keep[query_block, query_block - j] == 1
+        kept = keep[step, query_block - step * (range_rows // BLOCK), query_block - j] == 1
         reaches = (j + 1) * BLOCK > first_start
         blocks[count] = j
         return count + jnp.where(kept & reaches, 1, 0)
@@ -90,8 +91,8 @@
             nt = (((1,), (1,)), ((), ()))
             s = lax.dot_general(keys, q, nt, preferred_element_type=f32)
             dp = lax.dot_general(values, g, nt, preferred_element_type=f32)
-            lse = stats_ref[0, 0:1, first : first + width]
-            delta = stats_ref[0, 1:2, first : first + width]
+            lse = stats_ref[0, 0, 0:1, first : first + width]
+            delta = stats_ref[0, 0, 1:2, first : first + width]
             probs = jnp.where(allowed, jnp.exp2(s * (scale * LOG2E) - lse), 0.0)
             dscores = probs * (dp - delta)
             probs_all.append(probs.astype(jnp.bfloat16))
@@ -126,27 +127,27 @@
 def attention(info, starts, keep, qg, stats, kv, range_rows):
     ranges, _, rows, columns = qg.shape
     parts = kv.shape[0]
+    chunks = stats.shape[1]
+    columns = columns // chunks
     span = parts * ranges * rows
     total = rows * columns // HD
     smem = pl.BlockSpec(memory_space=pltpu.SMEM)
     f32, bf16 = jnp.float32, jnp.bfloat16
+    kv_spec = pl.BlockSpec((parts, ranges, 2, rows, HD), lambda c, t: (0, 0, 0, 0, c))
     return pl.pallas_call(
         functools.partial(attention_kernel, range_rows),
-        grid=(ranges,),
+        grid=(chunks, ranges),
         out_shape=(
-            jax.ShapeDtypeStruct((ranges, rows, columns), bf16),
+            jax.ShapeDtypeStruct((ranges, rows, columns * chunks), bf16),
             jax.ShapeDtypeStruct(kv.shape, bf16),
         ),
         in_specs=[
             smem, smem, smem,
-            pl.BlockSpec((1, 2, rows, columns), lambda t: (t, 0, 0, 0)),
-            pl.BlockSpec((1, 2, total), lambda t: (t, 0, 0)),
-            pl.BlockSpec(kv.shape, lambda t: (0, 0, 0, 0, 0)),
+            pl.BlockSpec((1, 2, rows, columns), lambda c, t: (t, 0, 0, c)),
+            pl.BlockSpec((1, 1, 2, total), lambda c, t: (t, c, 0, 0)),
+            kv_spec,
         ],
-        out_specs=(
-            pl.BlockSpec((1, rows, columns), lambda t: (t, 0, 0)),
-            pl.BlockSpec(kv.shape, lambda t: (0, 0, 0, 0, 0)),
-        ),
+        out_specs=(pl.BlockSpec((1, rows, columns), lambda c, t: (t, 0, c)), kv_spec),
         scratch_shapes=[
             pltpu.VMEM((span, HD), bf16),
             pltpu.VMEM((span, HD), bf16),
@@ -158,65 +159,268 @@
         ],
         compiler_params=pltpu.CompilerParams(vmem_limit_bytes=40 * 1024 * 1024),
         cost_estimate=pl.CostEstimate(
-            flops=5 * 2 * total * span * HD * ranges // 2,
-            bytes_accessed=3 * ranges * rows * columns * 2 + 4 * span * HD * 2,
-            transcendentals=total * span * ranges // 2,
+            flops=5 * 2 * total * span * HD * ranges * chunks // 2,
+            bytes_accessed=(3 * ranges * rows * columns * 2 + 4 * span * HD * 2) * chunks,
+            transcendentals=total * span * ranges * chunks // 2,
         ),
     )(info, starts, keep, qg, stats, kv)
 
 
+def place(ranges):
+    blk, sub = lax.axis_index("blk"), lax.axis_index("head")
+    mine = blk % ranges
+    return blk - mine, mine, sub
+
+
+def enter(base, mine, sub, ranges, parts):
+    barrier = pltpu.get_barrier_semaphore()
+    for d in range(1, ranges):
+        peer = (base + (mine + d) % ranges, sub)
+        pl.semaphore_signal(barrier, inc=1, device_id=peer, device_id_type=MESH)
+    for d in range(1, parts):
+        peer = (base + mine, (sub + d) % parts)
+        pl.semaphore_signal(barrier, inc=1, device_id=peer, device_id_type=MESH)
+    pl.semaphore_wait(barrier, ranges - 1 + parts - 1)
+
+
+def exchange_in_kernel(
+    ranges, parts, query, key, value, output, out_grad, lse_t, block_keep,
+    qg, stats, kv, keep,
+    g_vmem, o_vmem, stats_own, local_sem, r_send, r_recv, z_send, z_recv,
+):
+    f32, bf16 = jnp.float32, jnp.bfloat16
+    rows = query.shape[0]
+    chunks = stats.shape[1]
+    group = lse_t.shape[0] // (ranges * chunks)
+    wide = query.shape[1] // ranges
+    narrow = key.shape[1] // ranges
+    base, mine, sub = place(ranges)
+    g_load = pltpu.make_async_copy(out_grad, g_vmem, local_sem.at[0])
+    o_load = pltpu.make_async_copy(output, o_vmem, local_sem.at[1])
+    g_load.start()
+    o_load.start()
+    enter(base, mine, sub, ranges, parts)
+
+    def cut(ref, r, size):
+        return ref.at[:, pl.ds(pl.multiple_of(r * size, size), size)]
+
+    def sends(kind, source, target):
+        out = []
+        for d in range(1, ranges):
+            peer = (mine + d) % ranges
+            out.append(
+                pltpu.make_async_remote_copy(
+                    src_ref=source(peer), dst_ref=target,
+                    send_sem=r_send.at[kind, d - 1], recv_sem=r_recv.at[kind, d - 1],
+                    device_id=(base + peer, sub), device_id_type=MESH,
+                )
+            )
+        own = pltpu.make_async_copy(source(mine), target, local_sem.at[2 + kind])
+        for copy in out:
+            copy.start()
+        own.start()
+        return out, own
+
+    k_out, k_own = sends(0, lambda r: cut(key, r, narrow), kv.at[sub, mine, 0])
+    v_out, v_own = sends(1, lambda r: cut(value, r, narrow), kv.at[sub, mine, 1])
+    q_out, q_own = sends(2, lambda r: cut(query, r, wide), qg.at[mine, 0])
+    g_out, g_own = sends(3, lambda r: cut(out_grad, r, wide), qg.at[mine, 1])
+    b_out, b_own = sends(4, lambda r: block_keep, keep.at[mine])
+
+    for copy in k_out + v_out:
+        copy.wait_recv()
+    k_own.wait()
+    v_own.wait()
+    gathers = []
+    for d in range(1, parts):
+        copy = pltpu.make_async_remote_copy(
+            src_ref=kv.at[sub], dst_ref=kv.at[sub],
+            send_sem=z_send.at[d - 1], recv_sem=z_recv.at[d - 1],
+            device_id=(base + mine, (sub + d) % parts), device_id_type=MESH,
+        )
+        copy.start()
+        gathers.append(copy)
+
+    g_load.wait()
+    o_load.wait()
+    ones = jnp.ones((8, 2 * HD), bf16)
+    for head in range(lse_t.shape[0]):
+        at = slice(head * HD, (head + 1) * HD)
+        product = g_vmem[:, at].astype(f32) * o_vmem[:, at].astype(f32)
+        high = product.astype(bf16)
+        low = (product - high.astype(f32)).astype(bf16)
+        both = jnp.concatenate([high, low], axis=1)
+        nt = (((1,), (1,)), ((), ()))
+        delta = lax.dot_general(ones, both, nt, preferred_element_type=f32)
+        r, c, h = head // (chunks * group), head // group % chunks, head % group
+        to = slice(h * rows, (h + 1) * rows)
+        stats_own[r, c, 0:1, to] = lse_t[head : head + 1, :]
+        stats_own[r, c, 1:2, to] = delta[0:1]
+    s_out, s_own = sends(5, lambda r: stats_own.at[r], stats.at[mine])
+
+    for copy in k_out + v_out:
+        copy.wait_send()
+    for copy in gathers + q_out + g_out + b_out + s_out:
+        copy.wait()
+    for own in (q_own, g_own, b_own, s_own):
+        own.wait()
+
+
+def exchange_in(query, key, value, output, out_grad, lse_t, block_keep, ranges, parts):
+    rows, width = query.shape
+    heads = lse_t.shape[0]
+    chunks = KVH // ranges
+    f32, bf16 = jnp.float32, jnp.bfloat16
+    anywhere = pl.BlockSpec(memory_space=pl.ANY)
+    dma = pltpu.SemaphoreType.DMA
+    return pl.pallas_call(
+        functools.partial(exchange_in_kernel, ranges, parts),
+        out_shape=(
+            jax.ShapeDtypeStruct((ranges, 2, rows, width // ranges), bf16),
+            jax.ShapeDtypeStruct((ranges, chunks, 2, heads // KVH * rows), f32),
+            jax.ShapeDtypeStruct((parts, ranges, 2, rows, key.shape[1] // ranges), bf16),
+            jax.ShapeDtypeStruct((ranges,) + block_keep.shape, jnp.int32),
+        ),
+        in_specs=[anywhere] * 5 + [pl.BlockSpec(memory_space=pltpu.VMEM), anywhere],
+        out_specs=(anywhere,) * 4,
+        scratch_shapes=[
+            pltpu.VMEM((rows, width), bf16),
+            pltpu.VMEM((rows, width), bf16),
+            pltpu.VMEM((ranges, chunks, 2, heads // KVH * rows), f32),
+            dma((8,)),
+            dma((6, ranges - 1)),
+            dma((6, ranges - 1)),
+            dma((parts - 1,)),
+            dma((parts - 1,)),
+        ],
+        compiler_params=pltpu.CompilerParams(
+            collective_id=0, has_side_effects=True, vmem_limit_bytes=40 * 1024 * 1024
+        ),
+    )(query, key, value, output, out_grad, lse_t, block_keep)
+
+
+def exchange_out_kernel(
+    ranges, parts, dq, dkv, query_grad, key_grad, value_grad,
+    partial, summed, local_sem, q_send, q_recv, r_send, r_recv, z_send, z_recv,
+):
+    f32, bf16 = jnp.float32, jnp.bfloat16
+    wide = query_grad.shape[1] // ranges
+    narrow = key_grad.shape[1] // ranges
+    base, mine, sub = place(ranges)
+    enter(base, mine, sub, ranges, parts)
+
+    def cut(ref, size):
+        return ref.at[:, pl.ds(pl.multiple_of(mine * size, size), size)]
+
+    own = pltpu.make_async_copy(dkv.at[sub], partial.at[sub], local_sem.at[0])
+    own.start()
+    pieces = []
+    for i in range(ranges):
+        row = []
+        t = i
+        for d in range(1, parts):
+            peer = (sub + d) % parts
+            copy = pltpu.make_async_remote_copy(
+                src_ref=dkv.at[peer, t], dst_ref=partial.at[sub, t],
+                send_sem=z_send.at[i, d - 1], recv_sem=z_recv.at[i, d - 1],
+                device_id=(base + mine, peer), device_id_type=MESH,
+            )
+            copy.start()
+            row.append(copy)
+        pieces.append(row)
+    out = []
+    for d in range(1, ranges):
+        peer = (mine + d) % ranges
+        copy = pltpu.make_async_remote_copy(
+            src_ref=dq.at[peer], dst_ref=cut(query_grad, wide),
+            send_sem=q_send.at[d - 1], recv_sem=q_recv.at[d - 1],
+            device_id=(base + peer, sub), device_id_type=MESH,
+        )
+        copy.start()
+        out.append(copy)
+    q_own = pltpu.make_async_copy(dq.at[mine], cut(query_grad, wide), local_sem.at[1])
+    q_own.start()
+    own.wait()
+    for i in range(ranges):
+        for copy in pieces[i]:
+            copy.wait_recv()
+        for part in range(2):
+            total = partial[0, i, part].astype(f32)
+            for z in range(1, parts):
+                total += partial[z, i, part].astype(f32)
+            summed[i, part] = total.astype(bf16)
+    owns = []
+    for part, grad in enumerate((key_grad, value_grad)):
+        for d in range(1, ranges):
+            peer = (mine + d) % ranges
+            copy = pltpu.make_async_remote_copy(
+                src_ref=summed.at[peer, part], dst_ref=cut(grad, narrow),
+                send_sem=r_send.at[part, d - 1], recv_sem=r_recv.at[part, d - 1],
+                device_id=(base + peer, sub), device_id_type=MESH,
+            )
+            copy.start()
+            out.append(copy)
+        grad_own = pltpu.make_async_copy(
+            summed.at[mine, part], cut(grad, narrow), local_sem.at[2 + part]
+        )
+        grad_own.start()
+        owns.append(grad_own)
+    for row in pieces:
+        for copy in row:
+            copy.wait_send()
+    for copy in out:
+        copy.wait()
+    q_own.wait()
+    for grad_own in owns:
+        grad_own.wait()
+
+
+def exchange_out(dq, dkv, ranges, parts):
+    _, rows, wide = dq.shape
+    narrow = dkv.shape[-1]
+    bf16 = jnp.bfloat16
+    anywhere = pl.BlockSpec(memory_space=pl.ANY)
+    dma = pltpu.SemaphoreType.DMA
+    return pl.pallas_call(
+        functools.partial(exchange_out_kernel, ranges, parts),
+        out_shape=(
+            jax.ShapeDtypeStruct((rows, wide * ranges), bf16),
+            jax.ShapeDtypeStruct((rows, narrow * ranges), bf16),
+            jax.ShapeDtypeStruct((rows, narrow * ranges), bf16),
+        ),
+        in_specs=[anywhere] * 2,
+        out_specs=(anywhere,) * 3,
+        scratch_shapes=[
+            pltpu.VMEM(dkv.shape, bf16),
+            pltpu.VMEM(dkv.shape[1:], bf16),
+            dma((4,)),
+            dma((ranges - 1,)),
+            dma((ranges - 1,)),
+            dma((2, ranges - 1)),
+            dma((2, ranges - 1)),
+            dma((ranges, parts - 1)),
+            dma((ranges, parts - 1)),
+        ],
+        compiler_params=pltpu.CompilerParams(
+            collective_id=1, has_side_effects=True, vmem_limit_bytes=40 * 1024 * 1024
+        ),
+    )(dq, dkv)
+
+
 def shards(query, key, value, output, out_grad, lse, doc_lengths, block_keep):
-    f32, bf16 = jnp.float32, jnp.bfloat16
     rows = query.shape[0]
     parts = lax.axis_size("head")
     range_rows = rows * parts
     ranges = DOC_MAX // range_rows
-    blks = lax.axis_size("blk")
-    groups = [[w + r for r in range(ranges)] for w in range(0, blks, ranges)]
-    chunks = KVH // ranges
-    heads = query.shape[1] // HD
-    group = heads // KVH
-    columns = group * HD
     sub = lax.axis_index("head")
     window = lax.axis_index("blk") // ranges
-
-    def swap(array):
-        return lax.all_to_all(array, "blk", 0, 0, axis_index_groups=groups)
-
     starts = (jnp.cumsum(doc_lengths) - doc_lengths - window * DOC_MAX).astype(jnp.int32)
     info = jnp.full((1,), sub * rows, jnp.int32)
-    keep = lax.all_gather(block_keep, "blk", axis_index_groups=groups, tiled=True)
-
-    q5 = query.reshape(rows, ranges, chunks, columns)
-    g5 = out_grad.reshape(rows, ranges, chunks, columns)
-    k5 = key.reshape(rows, ranges, chunks, HD)
-    v5 = value.reshape(rows, ranges, chunks, HD)
-    kv_in, qg_in = [], []
-    for c in range(chunks):
-        kv = jnp.stack([k5[:, :, c], v5[:, :, c]], axis=0).transpose(2, 0, 1, 3)
-        kv_in.append(lax.all_gather(swap(kv), "head"))
-        qg = jnp.stack([q5[:, :, c], g5[:, :, c]], axis=0).transpose(2, 0, 1, 3)
-        qg_in.append(swap(qg))
-    delta = jnp.sum(
-        out_grad.reshape(rows, heads, HD).astype(f32) * output.reshape(rows, heads, HD).astype(f32),
-        axis=2,
+    qg, stats, kv, keep = exchange_in(
+        query, key, value, output, out_grad, (lse * LOG2E).T, block_keep, ranges, parts
     )
-    stats = jnp.stack([lse * LOG2E, delta], axis=0)
-    stats = stats.reshape(2, rows, ranges, chunks, group).transpose(2, 3, 0, 4, 1)
-    stats = swap(stats.reshape(ranges, chunks, 2, group * rows))
-
-    dq_out, dkv_out = [], []
-    for c in range(chunks):
-        dq, dkv = attention(info, starts, keep, qg_in[c], stats[:, c], kv_in[c], range_rows)
-        dq_out.append(swap(dq))
-        partial = lax.all_to_all(dkv, "head", 0, 0)
-        summed = jnp.sum(partial.astype(f32), axis=0).astype(bf16)
-        dkv_out.append(swap(summed))
-    query_grad = jnp.stack(dq_out, axis=1).transpose(2, 0, 1, 3).reshape(rows, heads * HD)
-    dkv = jnp.stack(dkv_out, axis=1)
-    key_grad = dkv[:, :, 0].transpose(2, 0, 1, 3).reshape(rows, KVH * HD)
-    value_grad = dkv[:, :, 1].transpose(2, 0, 1, 3).reshape(rows, KVH * HD)
-    return (query_grad, key_grad, value_grad)
+    dq, dkv = attention(info, starts, keep, qg, stats, kv, range_rows)
+    return exchange_out(dq, dkv, ranges, parts)
 
 
 def solution(mesh):

time: 259 us -> 158 us (0.61)
  the two profiles are of different devices: /device:TPU:7 before, /device:TPU:15 now
where the time goes in v2:
time: 158 us; the launch traced here: 157 us
  Pallas kernels  144 us (91%)
  local copies, waits for them, and re-layouts  10.1 us (6%)
  other arithmetic  2.25 us (1%)
    pallas_call x1, Pallas kernels, exchange_out(): pl.pallas_call(functools.partial(exchange_out_kernel, ranges, parts), out...  63.7 us
    pallas_call x1, Pallas kernels, exchange_in(): pl.pallas_call(functools.partial(exchange_in_kernel, ranges, parts), out_...  56.7 us
    pallas_call x1, Pallas kernels, attention(): pl.pallas_call(functools.partial(attention_kernel, range_rows), grid=(chu...  23.8 us
    unnamed x15, local copies, waits for them, and re-layouts  10.1 us

profile of v2, /device:TPU:15, one launch (start us, length us, event | category | flops | bytes accessed | tf_op | source)
XLA Modules:
  0.0 157.3 jit_solution(8230814054429426893)
XLA Ops:
  0.6 0.8 reduce-window.9
  1.5 0.7 fusion.starts
  2.1 0.8 multiply_bitcast_fusion.lse_t
  2.9 0.0 copy-start
  2.9 1.6 %copy-done = bf16[128,8192]{1,0:T(8,128)(2,1)S(1)} copy-done((bf16[128,8192]{1,0:T(8,128)(2,1)S(1)}, bf16[128,8192]{1,0:T(8,128)(2,1)}, u32[]{:S(2)}) %copy-start) | copy-done | bytes 2097176
  4.5 0.0 copy-start.1
  4.5 1.6 %copy-done.1 = bf16[128,8192]{1,0:T(8,128)(2,1)S(1)} copy-done((bf16[128,8192]{1,0:T(8,128)(2,1)S(1)}, bf16[128,8192]{1,0:T(8,128)(2,1)}, u32[]{:S(2)}) %copy-start.1) | copy-done | bytes 2097176
  6.1 0.0 copy-start.2
  6.1 1.6 %copy-done.2 = bf16[128,8192]{1,0:T(8,128)(2,1)S(1)} copy-done((bf16[128,8192]{1,0:T(8,128)(2,1)S(1)}, bf16[128,8192]{1,0:T(8,128)(2,1)}, u32[]{:S(2)}) %copy-start.2) | copy-done | bytes 2097176
  7.7 0.0 copy-start.3
  7.7 0.9 copy-done.3
  8.6 0.0 copy-start.4
  8.6 0.9 copy-done.4
  9.6 0.0 copy-start.5
  9.6 0.7 copy-done.5
  10.3 56.7 %shard_map.103 = (bf16[4,2,128,2048]{3,2,1,0:T(8,128)(2,1)S(1)}, f32[4,2,2,1024]{3,2,1,0:T(2,128)S(1)}, bf16[4,4,2,128,256]{4,3,2,1,0:T(8,128)(2,1)S(1)}, s32[4,4,17]{2,1,0:T(4,128)S(1)}) custom-call(bf16[128,8192]{1,0:T(8,128)(2,1)S(1)} %copy-done, bf16[128,1024]{1,0:T(8,128)(2,1)S(1)} %copy-done.3, bf16[128,1024]{1,0:T(8,128)(2,1)S(1)} %copy-done.4, ...), custom_call_target="tpu_custom_call" | custom-call | tf_op jit(solution)/shard_map/pallas_call | solution.py:276
  67.0 23.8 %shard_map.104 = (bf16[4,128,2048]{2,1,0:T(8,128)(2,1)S(1)}, bf16[4,4,2,128,256]{4,3,2,1,0:T(8,128)(2,1)S(1)}) custom-call(s32[1]{0:T(128)} %bitcast.info, s32[3]{0:T(128)S(1)} %fusion.starts, s32[4,4,17]{2,1,0:T(4,128)S(1)} %get-tuple-element.9.keep, bf16[4,2,128,2048]{3,2,1,0:T(8,128)(2,1)S(1)} %get-tuple-element.10.qg_ref, ...), custom_call_target="tpu_custom_call" | custom-call | flops 10737418240 | bytes 10485760 | tf_op jit(solution)/shard_map/pallas_call | solution.py:137
  90.8 63.7 %shard_map.105 = (bf16[128,8192]{1,0:T(8,128)(2,1)S(1)}, bf16[128,1024]{1,0:T(8,128)(2,1)S(1)}, bf16[128,1024]{1,0:T(8,128)(2,1)S(1)}) custom-call(bf16[4,128,2048]{2,1,0:T(8,128)(2,1)S(1)} %get-tuple-element.13.dq, bf16[4,4,2,128,256]{4,3,2,1,0:T(8,128)(2,1)S(1)} %get-tuple-element.14.dkv), custom_call_target="tpu_custom_call" | custom-call | tf_op jit(solution)/shard_map/pallas_call | solution.py:384
  154.6 1.3 copy.14
  155.9 0.7 copy.15
  156.6 0.7 copy.16
Async XLA Ops:
  2.9 1.6 %copy-start = (bf16[128,8192]{1,0:T(8,128)(2,1)S(1)}, bf16[128,8192]{1,0:T(8,128)(2,1)}, u32[]{:S(2)}) copy-start(bf16[128,8192]{1,0:T(8,128)(2,1)} %query.1) | copy-start | bytes 6291460
  4.5 1.6 %copy-start.1 = (bf16[128,8192]{1,0:T(8,128)(2,1)S(1)}, bf16[128,8192]{1,0:T(8,128)(2,1)}, u32[]{:S(2)}) copy-start(bf16[128,8192]{1,0:T(8,128)(2,1)} %output.1) | copy-start | bytes 6291460
  6.1 1.6 %copy-start.2 = (bf16[128,8192]{1,0:T(8,128)(2,1)S(1)}, bf16[128,8192]{1,0:T(8,128)(2,1)}, u32[]{:S(2)}) copy-start(bf16[128,8192]{1,0:T(8,128)(2,1)} %out_grad.1) | copy-start | bytes 6291460
  7.7 0.9 copy-start.3
  8.6 0.9 copy-start.4
  9.6 0.7 copy-start.5

commit v3 on v1

v3 whole, which is shorter than its diff:
```python
import functools
import math

import jax
import jax.numpy as jnp
from jax import lax
from jax.experimental import pallas as pl
from jax.experimental.pallas import tpu as pltpu
from jax.sharding import PartitionSpec as P

KVH = 8
HD = 128
DOC_MAX = 2048
BLOCK = 128
LOG2E = 1.4426950408889634
FAR = 1 << 20
MESH = pl.DeviceIdType.MESH


def place(ranges):
    blk, sub = lax.axis_index("blk"), lax.axis_index("head")
    mine = blk % ranges
    return blk - mine, mine, sub


def enter(base, mine, sub, ranges, parts):
    barrier = pltpu.get_barrier_semaphore()
    for d in range(1, ranges):
        peer = (base + (mine + d) % ranges, sub)
        pl.semaphore_signal(barrier, inc=1, device_id=peer, device_id_type=MESH)
    for d in range(1, parts):
        peer = (base + mine, (sub + d) % parts)
        pl.semaphore_signal(barrier, inc=1, device_id=peer, device_id_type=MESH)
    pl.semaphore_wait(barrier, ranges - 1 + parts - 1)


def whole_kernel(
    ranges, parts, starts, query, key, value, output, out_grad, lse_t, block_keep,
    query_grad, key_grad, value_grad,
    g_vmem, o_vmem, stats_own, stats, qg, kv, keep_in, keep,
    k_all, v_all, kt_all, dk_acc, dv_acc, dqt_acc, dq_out, dkv_out, partial, summed,
    local, r_send, r_recv, z_send, z_recv, q_send, q_recv, p_send, p_recv, f_send, f_recv,
):
    f32, bf16 = jnp.float32, jnp.bfloat16
    rows = query.shape[0]
    chunks = stats.shape[1]
    group = lse_t.shape[0] // (ranges * chunks)
    columns = group * HD
    total = group * rows
    width = min(total, 256)
    span = k_all.shape[0]
    range_rows = rows * parts
    scale = 1.0 / math.sqrt(HD)
    nt = (((1,), (1,)), ((), ()))
    base, mine, sub = place(ranges)
    offset = sub * rows
    keep_row = offset // BLOCK

    g_load = pltpu.make_async_copy(out_grad, g_vmem, local.at[0])
    o_load = pltpu.make_async_copy(output, o_vmem, local.at[1])
    g_load.start()
    o_load.start()
    enter(base, mine, sub, ranges, parts)

    def cut(ref, r, c, size):
        first = pl.multiple_of((r * chunks + c) * size, size)
        return ref.at[:, pl.ds(first, size)]

    def sends(kind, source, target):
        out = []
        for d in range(1, ranges):
            peer = (mine + d) % ranges
            out.append(
                pltpu.make_async_remote_copy(
                    src_ref=source(peer), dst_ref=target,
                    send_sem=r_send.at[kind, d - 1], recv_sem=r_recv.at[kind, d - 1],
                    device_id=(base + peer, sub), device_id_type=MESH,
                )
            )
        own = pltpu.make_async_copy(source(mine), target, local.at[2 + kind])
        for copy in out:
            copy.start()
        own.start()
        return out + [own]

    def kv_sends(c):
        return sends(4 * c, lambda r: cut(key, r, c, HD), kv.at[c, sub, mine, 0]) + sends(
            4 * c + 1, lambda r: cut(value, r, c, HD), kv.at[c, sub, mine, 1]
        )

    def qg_sends(c):
        return sends(4 * c + 2, lambda r: cut(query, r, c, columns), qg.at[c, mine, 0]) + sends(
            4 * c + 3, lambda r: cut(out_grad, r, c, columns), qg.at[c, mine, 1]
        )

    def gather(c):
        out = []
        for d in range(1, parts):
            copy = pltpu.make_async_remote_copy(
                src_ref=kv.at[c, sub], dst_ref=kv.at[c, sub],
                send_sem=z_send.at[c, d - 1], recv_sem=z_recv.at[c, d - 1],
                device_id=(base + mine, (sub + d) % parts), device_id_type=MESH,
            )
            copy.start()
            out.append(copy)
        return out

    def wait(copies):
        for copy in copies:
            copy.wait()

    kv_moves = [kv_sends(c) for c in range(chunks)]
    keep_moves = sends(4 * chunks + 1, lambda r: block_keep, keep_in.at[mine])
    qg_moves = [qg_sends(0)] + [None] * (chunks - 1)
    wait(kv_moves[0])
    gathers = [gather(0)] + [None] * (chunks - 1)

    g_load.wait()
    o_load.wait()
    ones = jnp.ones((8, 2 * HD), bf16)
    for head in range(lse_t.shape[0]):
        at = slice(head * HD, (head + 1) * HD)
        product = g_vmem[:, at].astype(f32) * o_vmem[:, at].astype(f32)
        high = product.astype(bf16)
        low = (product - high.astype(f32)).astype(bf16)
        both = jnp.concatenate([high, low], axis=1)
        delta = lax.dot_general(ones, both, nt, preferred_element_type=f32)
        r, c, h = head // (chunks * group), head // group % chunks, head % group
        to = slice(h * rows, (h + 1) * rows)
        stats_own[r, c, 0:1, to] = lse_t[head : head + 1, :]
        stats_own[r, c, 1:2, to] = delta[0:1]
    stats_moves = sends(4 * chunks, lambda r: stats_own.at[r], stats.at[mine])

    wait(keep_moves)
    keep_copy = pltpu.make_async_copy(keep_in, keep, local.at[0])
    keep_copy.start()
    keep_copy.wait()
    for c in range(1, chunks):
        wait(kv_moves[c])
    wait(stats_moves)

    def doc_start(position):
        found = jnp.zeros_like(position)
        for d in range(starts.shape[0]):
            found = jnp.maximum(found, jnp.where(starts[d] <= position, starts[d], 0))
        return found

    def compute(c, t):
        first_query = t * range_rows + offset
        query_block = first_query // BLOCK
        row_query = first_query + lax.broadcasted_iota(jnp.int32, (1, width), 1) % rows
        row_start = doc_start(row_query)
        heads = range(group)
        queries = [qg[c, t, 0, :, h * HD : (h + 1) * HD] for h in heads]
        grads = [qg[c, t, 1, :, h * HD : (h + 1) * HD] for h in heads]
        queries = jnp.concatenate(queries, axis=0)
        grads = jnp.concatenate(grads, axis=0)
        dqt_acc[...] = jnp.zeros_like(dqt_acc)

        def pair(p, _):
            j = 2 * p
            at = pl.ds(pl.multiple_of(j * BLOCK, 2 * BLOCK), 2 * BLOCK)
            keys, values, keys_t = k_all[at, :], v_all[at, :], kt_all[:, at]
            drop0 = (1 - keep[t, keep_row, query_block - j]) * FAR
            drop1 = (1 - keep[t, keep_row, jnp.maximum(query_block - j - 1, 0)]) * FAR
            line = lax.broadcasted_iota(jnp.int32, (2 * BLOCK, width), 0)
            key_pos = line + j * BLOCK + jnp.where(line < BLOCK, drop0, drop1)
            allowed = (key_pos <= row_query) & (key_pos >= row_start)
            probs_all, dscores_all = [], []
            for first in range(0, total, width):
                q = queries[first : first + width]
                g = grads[first : first + width]
                s = lax.dot_general(keys, q, nt, preferred_element_type=f32)
                dp = lax.dot_general(values, g, nt, preferred_element_type=f32)
                lse = stats[t, c, 0:1, first : first + width]
                delta = stats[t, c, 1:2, first : first + width]
                probs = jnp.where(allowed, jnp.exp2(s * (scale * LOG2E) - lse), 0.0)
                dscores = probs * (dp - delta)
                probs_all.append(probs.astype(bf16))
                dscores_all.append(dscores.astype(bf16))
            probs_all = jnp.concatenate(probs_all, axis=1)
            dscores_all = jnp.concatenate(dscores_all, axis=1)
            dv_acc[at, :] += jnp.dot(probs_all, grads, preferred_element_type=f32)
            dk_acc[at, :] += jnp.dot(dscores_all, queries, preferred_element_type=f32)
            dqt_acc[...] += jnp.dot(keys_t, dscores_all, preferred_element_type=f32)
            return 0

        lax.fori_loop(0, (query_block + 2) // 2, pair, 0)
        for first in range(0, total, width):
            dq = (dqt_acc[:, first : first + width] * scale).T.astype(bf16)
            for h in range(width // rows):
                head = first // rows + h
                dq_out[c, t, :, head * HD : (head + 1) * HD] = dq[h * rows : (h + 1) * rows]
        for z in range(parts):
            first = (t * parts + z) * rows
            dkv_out[c, t, z, 0] = (dk_acc[first : first + rows, :] * scale).astype(bf16)
            dkv_out[c, t, z, 1] = dv_acc[first : first + rows, :].astype(bf16)

    def to_range(t, source, ref, c, size, send, recv, own):
        remote = pltpu.make_async_remote_copy(
            src_ref=source, dst_ref=cut(ref, mine, c, size),
            send_sem=send.at[t], recv_sem=recv.at[mine],
            device_id=(base + t, sub), device_id_type=MESH,
        )
        here = pltpu.make_async_copy(source, cut(ref, mine, c, size), own)

        @pl.when(t != mine)
        def _():
            remote.start()

        @pl.when(t == mine)
        def _():
            here.start()

        def finish():
            @pl.when(t != mine)
            def _():
                remote.wait_send()
                pltpu.make_async_remote_copy(
                    src_ref=source, dst_ref=cut(ref, t, c, size),
                    send_sem=send.at[t], recv_sem=recv.at[t],
                    device_id=(base + t, sub), device_id_type=MESH,
                ).wait_recv()

            @pl.when(t == mine)
            def _():
                here.wait()

        return finish

    def send_partial(c, t):
        out = []
        for d in range(1, parts):
            peer = (sub + d) % parts
            copy = pltpu.make_async_remote_copy(
                src_ref=dkv_out.at[c, t, peer], dst_ref=partial.at[c, t, d - 1],
                send_sem=p_send.at[c, t, d - 1], recv_sem=p_recv.at[c, t, d - 1],
                device_id=(base + mine, peer), device_id_type=MESH,
            )
            copy.start()
            out.append(copy)
        return out

    def add_up(c, t):
        for copy in partials[c, t]:
            copy.wait_recv()
        for part in range(2):
            sums = dkv_out[c, t, sub, part].astype(f32)
            for d in range(parts - 1):
                sums += partial[c, t, d, part].astype(f32)
            summed[c, t, part] = sums.astype(bf16)
        for part, ref in enumerate((key_grad, value_grad)):
            finishes.append(
                to_range(
                    t, summed.at[c, t, part], ref, c, HD,
                    f_send.at[c, part], f_recv.at[c, part], local.at[16 + 2 * c + part],
                )
            )

    partials, finishes = {}, []
    order = list(range(ranges - 1, -1, -1))
    for c in range(chunks):
        wait(qg_moves[c])
        wait(gathers[c])
        if c + 1 < chunks:
            qg_moves[c + 1] = qg_sends(c + 1)
            gathers[c + 1] = gather(c + 1)
        for t in range(ranges):
            for z in range(parts):
                first = (t * parts + z) * rows
                k_all[first : first + rows, :] = kv[c, z, t, 0]
                v_all[first : first + rows, :] = kv[c, z, t, 1]
        for first in range(0, span, 256):
            piece = k_all[first : first + 256, :].astype(f32)
            kt_all[:, first : first + 256] = piece.T.astype(bf16)
        dk_acc[...] = jnp.zeros_like(dk_acc)
        dv_acc[...] = jnp.zeros_like(dv_acc)
        for t in order:
            compute(c, t)
            partials[c, t] = send_partial(c, t)
            finishes.append(
                to_range(
                    t, dq_out.at[c, t], query_grad, c, columns,
                    q_send.at[c], q_recv.at[c], local.at[12 + c],
                )
            )
            if c > 0:
                add_up(c - 1, t)
    for t in order:
        add_up(chunks - 1, t)
    for copies in partials.values():
        for copy in copies:
            copy.wait_send()
    for finish in finishes:
        finish()


def shards(query, key, value, output, out_grad, lse, doc_lengths, block_keep):
    rows, wide = query.shape
    narrow = key.shape[1]
    parts = lax.axis_size("head")
    range_rows = rows * parts
    ranges = DOC_MAX // range_rows
    chunks = KVH // ranges
    columns = wide // KVH
    total = columns // HD * rows
    window = lax.axis_index("blk") // ranges
    starts = (jnp.cumsum(doc_lengths) - doc_lengths - window * DOC_MAX).astype(jnp.int32)
    f32, bf16 = jnp.float32, jnp.bfloat16
    anywhere = pl.BlockSpec(memory_space=pl.ANY)
    vmem, dma = pltpu.VMEM, pltpu.SemaphoreType.DMA
    kinds = 4 * chunks + 2
    return pl.pallas_call(
        functools.partial(whole_kernel, ranges, parts),
        out_shape=(
            jax.ShapeDtypeStruct((rows, wide), bf16),
            jax.ShapeDtypeStruct((rows, narrow), bf16),
            jax.ShapeDtypeStruct((rows, narrow), bf16),
        ),
        in_specs=[pl.BlockSpec(memory_space=pltpu.SMEM)]
        + [anywhere] * 5
        + [pl.BlockSpec(memory_space=pltpu.VMEM), anywhere],
        out_specs=(anywhere,) * 3,
        scratch_shapes=[
            vmem((rows, wide), bf16),
            vmem((rows, wide), bf16),
            vmem((ranges, chunks, 2, total), f32),
            vmem((ranges, chunks, 2, total), f32),
            vmem((chunks, ranges, 2, rows, columns), bf16),
            vmem((chunks, parts, ranges, 2, rows, HD), bf16),
            vmem((ranges,) + block_keep.shape, jnp.int32),
            pltpu.SMEM((ranges,) + block_keep.shape, jnp.int32),
            vmem((DOC_MAX, HD), bf16),
            vmem((DOC_MAX, HD), bf16),
            vmem((HD, DOC_MAX), bf16),
            vmem((DOC_MAX, HD), f32),
            vmem((DOC_MAX, HD), f32),
            vmem((HD, total), f32),
            vmem((chunks, ranges, rows, columns), bf16),
            vmem((chunks, ranges, parts, 2, rows, HD), bf16),
            vmem((chunks, ranges, parts - 1, 2, rows, HD), bf16),
            vmem((chunks, ranges, 2, rows, HD), bf16),
            dma((20,)),
            dma((kinds, ranges - 1)),
            dma((kinds, ranges - 1)),
            dma((chunks, parts - 1)),
            dma((chunks, parts - 1)),
            dma((chunks, ranges)),
            dma((chunks, ranges)),
            dma((chunks, ranges, parts - 1)),
            dma((chunks, ranges, parts - 1)),
            dma((chunks, 2, ranges)),
            dma((chunks, 2, ranges)),
        ],
        compiler_params=pltpu.CompilerParams(
            collective_id=0, has_side_effects=True, vmem_limit_bytes=60 * 1024 * 1024
        ),
        cost_estimate=pl.CostEstimate(
            flops=10 * total * DOC_MAX * HD * ranges * chunks // 2,
            bytes_accessed=7 * rows * wide * 2,
            transcendentals=total * DOC_MAX * ranges * chunks // 2,
        ),
    )(starts, query, key, value, output, out_grad, (lse * LOG2E).T, block_keep)


def solution(mesh):
    tokens = P(("blk", "head"), None)
    in_specs = (tokens, tokens, tokens, tokens, tokens, tokens, P(), P("blk", None))
    out_specs = (tokens, tokens, tokens)
    return jax.shard_map(shards, mesh=mesh, in_specs=in_specs, out_specs=out_specs, check_vma=False)
```

time: 259 us -> 119 us (0.46)
  the two profiles are of different devices: /device:TPU:7 before, /device:TPU:0 now
where the time goes in v3:
time: 119 us
  Pallas kernels  110 us (92%)
  local copies, waits for them, and re-layouts  4.56 us (4%)
  other arithmetic  3.37 us (3%)
    pallas_call x1, Pallas kernels, shards(): pl.pallas_call(functools.partial(whole_kernel, ranges, parts), out_shape=...  110 us
    unnamed x7, local copies, waits for them, and re-layouts  4.56 us

profile of v3, /device:TPU:0, one launch (start us, length us, event | category | flops | bytes accessed | tf_op | source)
XLA Modules:
  0.0 118.7 jit_solution(8770259433733811823)
XLA Ops:
  0.6 0.8 reduce-window.9
  1.5 1.2 fusion.starts
  2.6 1.4 %multiply_bitcast_fusion.lse_t = f32[64,128]{1,0:T(8,128)} fusion(f32[128,64]{0,1:T(8,128)} %param.13), kind=kLoop, calls=%fused_computation | loop fusion | flops 8192 | bytes 65536 | tf_op jit(solution)/shard_map/transpose | solution.py:363
  4.0 110.1 %shard_map.103 = (bf16[128,8192]{1,0:T(8,128)(2,1)}, bf16[128,1024]{1,0:T(8,128)(2,1)}, bf16[128,1024]{1,0:T(8,128)(2,1)}) custom-call(s32[3]{0:T(128)} %fusion.starts, bf16[128,8192]{1,0:T(8,128)(2,1)} %query.1, bf16[128,1024]{1,0:T(8,128)(2,1)} %key.1, bf16[128,1024]{1,0:T(8,128)(2,1)} %value.1, bf16[128,8192]{1,0:T(8,128)(2,1)} %output.1, ...), custom_call_target="tpu_custom_call" | custom-call | flops 10737418240 | bytes 14680064 | tf_op jit(solution)/shard_map/pallas_call | solution.py:313
  114.1 0.0 copy-start.1
  114.1 0.0 copy-start
  114.1 3.2 %copy.14 = bf16[128,8192]{1,0:T(8,128)(2,1)} copy(bf16[128,8192]{1,0:T(8,128)(2,1)} %get-tuple-element.6) | data formatting | bytes 4194304
  117.3 0.0 copy-done.1
  117.3 0.7 copy.15
  118.0 0.0 copy-done
  118.0 0.7 copy.16
Async XLA Ops:
  114.1 3.2 %copy-start.1 = (bf16[128,1024]{1,0:T(8,128)(2,1)S(1)}, bf16[128,1024]{1,0:T(8,128)(2,1)}, u32[]{:S(2)}) copy-start(bf16[128,1024]{1,0:T(8,128)(2,1)} %get-tuple-element.7) | copy-start | bytes 786436
  114.1 3.9 %copy-start = (bf16[128,1024]{1,0:T(8,128)(2,1)S(1)}, bf16[128,1024]{1,0:T(8,128)(2,1)}, u32[]{:S(2)}) copy-start(bf16[128,1024]{1,0:T(8,128)(2,1)} %get-tuple-element.8) | copy-start | bytes 786436

commit v4 on v3

--- a/solution.py
+++ b/solution.py
@@ -40,11 +40,15 @@
     g_vmem, o_vmem, stats_own, stats, qg, kv, keep_in, keep,
     k_all, v_all, kt_all, dk_acc, dv_acc, dqt_acc, dq_out, dkv_out, partial, summed,
     local, r_send, r_recv, z_send, z_recv, q_send, q_recv, p_send, p_recv, f_send, f_recv,
+    relayed, relay_send, relay_recv, q_own, f_own,
 ):
     f32, bf16 = jnp.float32, jnp.bfloat16
     rows = query.shape[0]
-    chunks = stats.shape[1]
-    group = lse_t.shape[0] // (ranges * chunks)
+    chunks = kv.shape[0]
+    units = stats.shape[1]
+    halves = units // chunks
+    group = lse_t.shape[0] // (ranges * units)
+    relay = parts == 4
     columns = group * HD
     total = group * rows
     width = min(total, 256)
@@ -63,7 +67,7 @@
     enter(base, mine, sub, ranges, parts)
 
     def cut(ref, r, c, size):
-        first = pl.multiple_of((r * chunks + c) * size, size)
+        first = pl.multiple_of(r * (ref.shape[1] // ranges) + c * size, size)
         return ref.at[:, pl.ds(first, size)]
 
     def sends(kind, source, target):
@@ -84,36 +88,108 @@
         return out + [own]
 
     def kv_sends(c):
-        return sends(4 * c, lambda r: cut(key, r, c, HD), kv.at[c, sub, mine, 0]) + sends(
-            4 * c + 1, lambda r: cut(value, r, c, HD), kv.at[c, sub, mine, 1]
+        return sends(2 * c, lambda r: cut(key, r, c, HD), kv.at[c, sub, mine, 0]) + sends(
+            2 * c + 1, lambda r: cut(value, r, c, HD), kv.at[c, sub, mine, 1]
         )
 
-    def qg_sends(c):
-        return sends(4 * c + 2, lambda r: cut(query, r, c, columns), qg.at[c, mine, 0]) + sends(
-            4 * c + 3, lambda r: cut(out_grad, r, c, columns), qg.at[c, mine, 1]
+    def qg_sends(u):
+        kind = 2 * chunks + 2 * u
+        return sends(kind, lambda r: cut(query, r, u, columns), qg.at[u, mine, 0]) + sends(
+            kind + 1, lambda r: cut(out_grad, r, u, columns), qg.at[u, mine, 1]
         )
 
+    def z_copy(src, dst, send, recv, z):
+        return pltpu.make_async_remote_copy(
+            src_ref=src, dst_ref=dst, send_sem=send, recv_sem=recv,
+            device_id=(base + mine, z), device_id_type=MESH,
+        )
+
+    def gather_copy(c, z, d, to, whole):
+        ref = kv.at[c, z] if whole else kv.at[c, z, pl.ds(0, ranges - 1)]
+        return z_copy(ref, ref, z_send.at[c, d - 1], z_recv.at[c, d - 1], to)
+
+    def forward_copy(c):
+        return z_copy(kv.at[c, 0], kv.at[c, 0], relay_send.at[c], z_recv.at[c, parts - 2], 3)
+
     def gather(c):
-        out = []
         for d in range(1, parts):
-            copy = pltpu.make_async_remote_copy(
-                src_ref=kv.at[c, sub], dst_ref=kv.at[c, sub],
-                send_sem=z_send.at[c, d - 1], recv_sem=z_recv.at[c, d - 1],
-                device_id=(base + mine, (sub + d) % parts), device_id_type=MESH,
-            )
-            copy.start()
-            out.append(copy)
-        return out
+            peer = (sub + d) % parts
+            far = relay and d == parts - 1
+
+            @pl.when((peer > sub) & (not far))
+            def _():
+                gather_copy(c, sub, d, peer, True).start()
+
+            @pl.when(peer < sub)
+            def _():
+                gather_copy(c, sub, d, peer, False).start()
+
+    def forward(c):
+        if relay:
+
+            @pl.when(sub == 2)
+            def _():
+                gather_copy(c, 0, 2, 3, True).wait_recv()
+                forward_copy(c).start()
+
+    def gathered(c):
+        for d in range(1, parts):
+            peer = (sub + d) % parts
+            origin = (sub - d + parts) % parts
+            far = relay and d == parts - 1
+            done = (sub == 2) & (relay and d == 2)
+
+            @pl.when((peer > sub) & (not far))
+            def _():
+                gather_copy(c, sub, d, peer, True).wait_send()
+
+            @pl.when(peer < sub)
+            def _():
+                gather_copy(c, sub, d, peer, False).wait_send()
+
+            @pl.when((origin < sub) & jnp.logical_not(done))
+            def _():
+                gather_copy(c, origin, d, peer, True).wait_recv()
+
+            @pl.when(origin > sub)
+            def _():
+                gather_copy(c, origin, d, peer, False).wait_recv()
+
+        if relay:
+
+            @pl.when(sub == 2)
+            def _():
+                forward_copy(c).wait_send()
 
     def wait(copies):
         for copy in copies:
             copy.wait()
 
     kv_moves = [kv_sends(c) for c in range(chunks)]
-    keep_moves = sends(4 * chunks + 1, lambda r: block_keep, keep_in.at[mine])
-    qg_moves = [qg_sends(0)] + [None] * (chunks - 1)
+    keep_moves = sends(2 * chunks + 2 * units + 1, lambda r: block_keep, keep_in.at[mine])
+    qg_moves = [qg_sends(0)] + [None] * (units - 1)
     wait(kv_moves[0])
-    gathers = [gather(0)] + [None] * (chunks - 1)
+    gather(0)
+    for c in range(chunks):
+        for z in range(1, parts):
+
+            @pl.when(z > sub)
+            def _():
+                kv[c, z, ranges - 1] = jnp.zeros(kv.shape[3:], bf16)
+
+        for d in range(1, parts):
+            origin = (sub - d + parts) % parts
+
+            @pl.when(origin < sub)
+            def _():
+                partial[c, ranges - 1, d - 1] = jnp.zeros(partial.shape[3:], bf16)
+
+        if relay:
+
+            @pl.when(sub == 0)
+            def _():
+                partial[c, :, 0] = jnp.zeros((ranges,) + partial.shape[3:], bf16)
+
 
     g_load.wait()
     o_load.wait()
@@ -125,12 +201,14 @@
         low = (product - high.astype(f32)).astype(bf16)
         both = jnp.concatenate([high, low], axis=1)
         delta = lax.dot_general(ones, both, nt, preferred_element_type=f32)
-        r, c, h = head // (chunks * group), head // group % chunks, head % group
+        r, c, h = head // (units * group), head // group % units, head % group
         to = slice(h * rows, (h + 1) * rows)
         stats_own[r, c, 0:1, to] = lse_t[head : head + 1, :]
         stats_own[r, c, 1:2, to] = delta[0:1]
-    stats_moves = sends(4 * chunks, lambda r: stats_own.at[r], stats.at[mine])
-
+    stats_moves = sends(2 * chunks + 2 * units, lambda r: stats_own.at[r], stats.at[mine])
+
+    qg_moves[1] = qg_sends(1)
+    forward(0)
     wait(keep_moves)
     keep_copy = pltpu.make_async_copy(keep_in, keep, local.at[0])
     keep_copy.start()
@@ -145,14 +223,14 @@
             found = jnp.maximum(found, jnp.where(starts[d] <= position, starts[d], 0))
         return found
 
-    def compute(c, t):
+    def compute(u, t):
         first_query = t * range_rows + offset
         query_block = first_query // BLOCK
         row_query = first_query + lax.broadcasted_iota(jnp.int32, (1, width), 1) % rows
         row_start = doc_start(row_query)
         heads = range(group)
-        queries = [qg[c, t, 0, :, h * HD : (h + 1) * HD] for h in heads]
-        grads = [qg[c, t, 1, :, h * HD : (h + 1) * HD] for h in heads]
+        queries = [qg[u, t, 0, :, h * HD : (h + 1) * HD] for h in heads]
+        grads = [qg[u, t, 1, :, h * HD : (h + 1) * HD] for h in heads]
         queries = jnp.concatenate(queries, axis=0)
         grads = jnp.concatenate(grads, axis=0)
         dqt_acc[...] = jnp.zeros_like(dqt_acc)
@@ -172,8 +250,8 @@
                 g = grads[first : first + width]
                 s = lax.dot_general(keys, q, nt, preferred_element_type=f32)
                 dp = lax.dot_general(values, g, nt, preferred_element_type=f32)
-                lse = stats[t, c, 0:1, first : first + width]
-                delta = stats[t, c, 1:2, first : first + width]
+                lse = stats[t, u, 0:1, first : first + width]
+                delta = stats[t, u, 1:2, first : first + width]
                 probs = jnp.where(allowed, jnp.exp2(s * (scale * LOG2E) - lse), 0.0)
                 dscores = probs * (dp - delta)
                 probs_all.append(probs.astype(bf16))
@@ -190,7 +268,9 @@
             dq = (dqt_acc[:, first : first + width] * scale).T.astype(bf16)
             for h in range(width // rows):
                 head = first // rows + h
-                dq_out[c, t, :, head * HD : (head + 1) * HD] = dq[h * rows : (h + 1) * rows]
+                dq_out[u, t, :, head * HD : (head + 1) * HD] = dq[h * rows : (h + 1) * rows]
+
+    def store(c, t):
         for z in range(parts):
             first = (t * parts + z) * rows
             dkv_out[c, t, z, 0] = (dk_acc[first : first + rows, :] * scale).astype(bf16)
@@ -228,22 +308,71 @@
 
         return finish
 
+    def partial_copy(c, t, d, peer):
+        return z_copy(
+            dkv_out.at[c, t, peer], partial.at[c, t, d - 1],
+            p_send.at[c, t, d - 1], p_recv.at[c, t, d - 1], peer,
+        )
+
+    def far_copy(c, t):
+        return z_copy(
+            dkv_out.at[c, t, 0], relayed.at[c, t],
+            p_send.at[c, t, 0], relay_recv.at[c, t], 2,
+        )
+
+    def is_sent(t, d, peer, origin):
+        sent = (peer < origin) | (t < ranges - 1)
+        if relay and d == 1:
+            sent = sent & (origin != 3)
+        return sent
+
     def send_partial(c, t):
-        out = []
         for d in range(1, parts):
             peer = (sub + d) % parts
-            copy = pltpu.make_async_remote_copy(
-                src_ref=dkv_out.at[c, t, peer], dst_ref=partial.at[c, t, d - 1],
-                send_sem=p_send.at[c, t, d - 1], recv_sem=p_recv.at[c, t, d - 1],
-                device_id=(base + mine, peer), device_id_type=MESH,
-            )
-            copy.start()
-            out.append(copy)
-        return out
+            late = (sub == 2) & (relay and d == 2)
+
+            @pl.when(is_sent(t, d, peer, sub) & jnp.logical_not(late))
+            def _():
+                partial_copy(c, t, d, peer).start()
+
+        if relay:
+
+            @pl.when(sub == 3)
+            def _():
+                far_copy(c, t).start()
+
+    def send_late(c, t):
+        if relay:
+
+            @pl.when(sub == 2)
+            def _():
+                far_copy(c, t).wait_recv()
+                both = dkv_out[c, t, 0].astype(f32) + relayed[c, t].astype(f32)
+                dkv_out[c, t, 0] = both.astype(bf16)
+                partial_copy(c, t, 2, 0).start()
+
+    def sent_partial(c, t):
+        for d in range(1, parts):
+            peer = (sub + d) % parts
+
+            @pl.when(is_sent(t, d, peer, sub))
+            def _():
+                partial_copy(c, t, d, peer).wait_send()
+
+        if relay:
+
+            @pl.when(sub == 3)
+            def _():
+                far_copy(c, t).wait_send()
 
     def add_up(c, t):
-        for copy in partials[c, t]:
-            copy.wait_recv()
+        for d in range(1, parts):
+            origin = (sub - d + parts) % parts
+
+            @pl.when(is_sent(t, d, sub, origin))
+            def _():
+                partial_copy(c, t, d, (sub + d) % parts).wait_recv()
+
         for part in range(2):
             sums = dkv_out[c, t, sub, part].astype(f32)
             for d in range(parts - 1):
@@ -253,44 +382,60 @@
             finishes.append(
                 to_range(
                     t, summed.at[c, t, part], ref, c, HD,
-                    f_send.at[c, part], f_recv.at[c, part], local.at[16 + 2 * c + part],
+                    f_send.at[c, part], f_recv.at[c, part], f_own.at[c, part],
                 )
             )
 
-    partials, finishes = {}, []
+    finishes = []
     order = list(range(ranges - 1, -1, -1))
-    for c in range(chunks):
-        wait(qg_moves[c])
-        wait(gathers[c])
-        if c + 1 < chunks:
-            qg_moves[c + 1] = qg_sends(c + 1)
-            gathers[c + 1] = gather(c + 1)
-        for t in range(ranges):
-            for z in range(parts):
-                first = (t * parts + z) * rows
-                k_all[first : first + rows, :] = kv[c, z, t, 0]
-                v_all[first : first + rows, :] = kv[c, z, t, 1]
-        for first in range(0, span, 256):
-            piece = k_all[first : first + 256, :].astype(f32)
-            kt_all[:, first : first + 256] = piece.T.astype(bf16)
-        dk_acc[...] = jnp.zeros_like(dk_acc)
-        dv_acc[...] = jnp.zeros_like(dv_acc)
-        for t in order:
-            compute(c, t)
-            partials[c, t] = send_partial(c, t)
+    late, ready = [], []
+    for u in range(units):
+        c = u // halves
+        wait(qg_moves[u])
+        if u % halves == 0:
+            gathered(c)
+            if c + 1 < chunks:
+                gather(c + 1)
+            for t in range(ranges):
+                for z in range(parts):
+                    first = (t * parts + z) * rows
+                    k_all[first : first + rows, :] = kv[c, z, t, 0]
+                    v_all[first : first + rows, :] = kv[c, z, t, 1]
+            for first in range(0, span, 256):
+                piece = k_all[first : first + 256, :].astype(f32)
+                kt_all[:, first : first + 256] = piece.T.astype(bf16)
+            dk_acc[...] = jnp.zeros_like(dk_acc)
+            dv_acc[...] = jnp.zeros_like(dv_acc)
+        for i, t in enumerate(order):
+            compute(u, t)
             finishes.append(
                 to_range(
-                    t, dq_out.at[c, t], query_grad, c, columns,
-                    q_send.at[c], q_recv.at[c], local.at[12 + c],
+                    t, dq_out.at[u, t], query_grad, u, columns,
+                    q_send.at[u], q_recv.at[u], q_own.at[u],
                 )
             )
-            if c > 0:
-                add_up(c - 1, t)
-    for t in order:
-        add_up(chunks - 1, t)
-    for copies in partials.values():
-        for copy in copies:
-            copy.wait_send()
+            if late:
+                at = late.pop(0)
+                send_late(*at)
+                ready.append(at)
+            if len(ready) > 3 or (ready and u % halves == 0):
+                add_up(*ready.pop(0))
+            if u % halves == halves - 1:
+                store(c, t)
+                send_partial(c, t)
+                late.append((c, t))
+            if i == 1 and u + 2 < units:
+                qg_moves[u + 2] = qg_sends(u + 2)
+            if i == ranges - 1 and u % halves == 0 and c + 1 < chunks:
+                forward(c + 1)
+    for at in late:
+        send_late(*at)
+        ready.append(at)
+    for at in ready:
+        add_up(*at)
+    for c in range(chunks):
+        for t in order:
+            sent_partial(c, t)
     for finish in finishes:
         finish()
 
@@ -302,14 +447,15 @@
     range_rows = rows * parts
     ranges = DOC_MAX // range_rows
     chunks = KVH // ranges
-    columns = wide // KVH
+    units = 2 * chunks
+    columns = wide // (ranges * units)
     total = columns // HD * rows
     window = lax.axis_index("blk") // ranges
     starts = (jnp.cumsum(doc_lengths) - doc_lengths - window * DOC_MAX).astype(jnp.int32)
     f32, bf16 = jnp.float32, jnp.bfloat16
     anywhere = pl.BlockSpec(memory_space=pl.ANY)
     vmem, dma = pltpu.VMEM, pltpu.SemaphoreType.DMA
-    kinds = 4 * chunks + 2
+    kinds = 2 * chunks + 2 * units + 2
     return pl.pallas_call(
         functools.partial(whole_kernel, ranges, parts),
         out_shape=(
@@ -324,9 +470,9 @@
         scratch_shapes=[
             vmem((rows, wide), bf16),
             vmem((rows, wide), bf16),
-            vmem((ranges, chunks, 2, total), f32),
-            vmem((ranges, chunks, 2, total), f32),
-            vmem((chunks, ranges, 2, rows, columns), bf16),
+            vmem((ranges, units, 2, total), f32),
+            vmem((ranges, units, 2, total), f32),
+            vmem((units, ranges, 2, rows, columns), bf16),
             vmem((chunks, parts, ranges, 2, rows, HD), bf16),
             vmem((ranges,) + block_keep.shape, jnp.int32),
             pltpu.SMEM((ranges,) + block_keep.shape, jnp.int32),
@@ -336,21 +482,26 @@
             vmem((DOC_MAX, HD), f32),
             vmem((DOC_MAX, HD), f32),
             vmem((HD, total), f32),
-            vmem((chunks, ranges, rows, columns), bf16),
+            vmem((units, ranges, rows, columns), bf16),
             vmem((chunks, ranges, parts, 2, rows, HD), bf16),
             vmem((chunks, ranges, parts - 1, 2, rows, HD), bf16),
             vmem((chunks, ranges, 2, rows, HD), bf16),
-            dma((20,)),
+            dma((2 + kinds,)),
             dma((kinds, ranges - 1)),
             dma((kinds, ranges - 1)),
             dma((chunks, parts - 1)),
             dma((chunks, parts - 1)),
-            dma((chunks, ranges)),
-            dma((chunks, ranges)),
+            dma((units, ranges)),
+            dma((units, ranges)),
             dma((chunks, ranges, parts - 1)),
             dma((chunks, ranges, parts - 1)),
             dma((chunks, 2, ranges)),
             dma((chunks, 2, ranges)),
+            vmem((chunks, ranges, 2, rows, HD), bf16),
+            dma((chunks,)),
+            dma((chunks, ranges)),
+            dma((units,)),
+            dma((chunks, 2)),
         ],
         compiler_params=pltpu.CompilerParams(
             collective_id=0, has_side_effects=True, vmem_limit_bytes=60 * 1024 * 1024

time: 119 us -> 117 us (0.983)
    pallas_call x1, Pallas kernels: 110 us -> 109 us  [shards(): pl.pallas_call(functools.partial(whole_kernel, ranges, parts), out_shape=...]
where the time goes in v4:
time: 117 us
  Pallas kernels  109 us (93%)
  local copies, waits for them, and re-layouts  4.56 us (4%)
  other arithmetic  3.37 us (3%)
    pallas_call x1, Pallas kernels, shards(): pl.pallas_call(functools.partial(whole_kernel, ranges, parts), out_shape=...  109 us
    unnamed x7, local copies, waits for them, and re-layouts  4.56 us

profile of v4, /device:TPU:0, one launch (start us, length us, event | category | flops | bytes accessed | tf_op | source)
XLA Modules:
  0.0 117.2 jit_solution(3383112859784510708)
XLA Ops:
  0.6 0.8 reduce-window.9
  1.5 1.2 fusion.starts
  2.6 1.4 %multiply_bitcast_fusion.lse_t = f32[64,128]{1,0:T(8,128)} fusion(f32[128,64]{0,1:T(8,128)} %param.13), kind=kLoop, calls=%fused_computation | loop fusion | flops 8192 | bytes 65536 | tf_op jit(solution)/shard_map/transpose | solution.py:514
  4.0 108.6 %shard_map.103 = (bf16[128,8192]{1,0:T(8,128)(2,1)}, bf16[128,1024]{1,0:T(8,128)(2,1)}, bf16[128,1024]{1,0:T(8,128)(2,1)}) custom-call(s32[3]{0:T(128)} %fusion.starts, bf16[128,8192]{1,0:T(8,128)(2,1)} %query.1, bf16[128,1024]{1,0:T(8,128)(2,1)} %key.1, bf16[128,1024]{1,0:T(8,128)(2,1)} %value.1, bf16[128,8192]{1,0:T(8,128)(2,1)} %output.1, ...), custom_call_target="tpu_custom_call" | custom-call | flops 5368709120 | bytes 14680064 | tf_op jit(solution)/shard_map/pallas_call | solution.py:459
  112.6 0.0 copy-start.1
  112.6 0.0 copy-start
  112.6 3.2 %copy.14 = bf16[128,8192]{1,0:T(8,128)(2,1)} copy(bf16[128,8192]{1,0:T(8,128)(2,1)} %get-tuple-element.6) | data formatting | bytes 4194304
  115.8 0.0 copy-done.1
  115.8 0.7 copy.15
  116.5 0.0 copy-done
  116.5 0.7 copy.16
Async XLA Ops:
  112.6 3.2 %copy-start.1 = (bf16[128,1024]{1,0:T(8,128)(2,1)S(1)}, bf16[128,1024]{1,0:T(8,128)(2,1)}, u32[]{:S(2)}) copy-start(bf16[128,1024]{1,0:T(8,128)(2,1)} %get-tuple-element.7) | copy-start | bytes 786436
  112.6 3.9 %copy-start = (bf16[128,1024]{1,0:T(8,128)(2,1)S(1)}, bf16[128,1024]{1,0:T(8,128)(2,1)}, u32[]{:S(2)}) copy-start(bf16[128,1024]{1,0:T(8,128)(2,1)} %get-tuple-element.8) | copy-start | bytes 786436

commit v5 on v4

--- a/solution.py
+++ b/solution.py
@@ -35,7 +35,7 @@
 
 
 def whole_kernel(
-    ranges, parts, starts, query, key, value, output, out_grad, lse_t, block_keep,
+    ranges, parts, lengths, query, key, value, output, out_grad, lse_t, block_keep,
     query_grad, key_grad, value_grad,
     g_vmem, o_vmem, stats_own, stats, qg, kv, keep_in, keep,
     k_all, v_all, kt_all, dk_acc, dv_acc, dqt_acc, dq_out, dkv_out, partial, summed,
@@ -207,7 +207,6 @@
         stats_own[r, c, 1:2, to] = delta[0:1]
     stats_moves = sends(2 * chunks + 2 * units, lambda r: stats_own.at[r], stats.at[mine])
 
-    qg_moves[1] = qg_sends(1)
     forward(0)
     wait(keep_moves)
     keep_copy = pltpu.make_async_copy(keep_in, keep, local.at[0])
@@ -219,8 +218,10 @@
 
     def doc_start(position):
         found = jnp.zeros_like(position)
-        for d in range(starts.shape[0]):
-            found = jnp.maximum(found, jnp.where(starts[d] <= position, starts[d], 0))
+        start = -(base // ranges) * DOC_MAX
+        for d in range(lengths.shape[0]):
+            found = jnp.maximum(found, jnp.where(start <= position, start, 0))
+            start = start + lengths[d]
         return found
 
     def compute(u, t):
@@ -389,9 +390,22 @@
     finishes = []
     order = list(range(ranges - 1, -1, -1))
     late, ready = [], []
+
+    def send_dq(u, t):
+        finishes.append(
+            to_range(
+                t, dq_out.at[u, t], query_grad, u, columns,
+                q_send.at[u], q_recv.at[u], q_own.at[u],
+            )
+        )
+
     for u in range(units):
         c = u // halves
         wait(qg_moves[u])
+        if u + 1 < units:
+            qg_moves[u + 1] = qg_sends(u + 1)
+        for held in order if u > 0 else ():
+            send_dq(u - 1, held)
         if u % halves == 0:
             gathered(c)
             if c + 1 < chunks:
@@ -408,25 +422,19 @@
             dv_acc[...] = jnp.zeros_like(dv_acc)
         for i, t in enumerate(order):
             compute(u, t)
-            finishes.append(
-                to_range(
-                    t, dq_out.at[u, t], query_grad, u, columns,
-                    q_send.at[u], q_recv.at[u], q_own.at[u],
-                )
-            )
-            if late:
-                at = late.pop(0)
-                send_late(*at)
-                ready.append(at)
-            if len(ready) > 3 or (ready and u % halves == 0):
-                add_up(*ready.pop(0))
+            if u == units - 1:
+                send_dq(u, t)
             if u % halves == halves - 1:
                 store(c, t)
                 send_partial(c, t)
                 late.append((c, t))
-            if i == 1 and u + 2 < units:
-                qg_moves[u + 2] = qg_sends(u + 2)
-            if i == ranges - 1 and u % halves == 0 and c + 1 < chunks:
+            if len(late) > 1:
+                at = late.pop(0)
+                send_late(*at)
+                ready.append(at)
+            if len(ready) > ranges - 1:
+                add_up(*ready.pop(0))
+            if i == 1 and u % halves == 0 and c + 1 < chunks:
                 forward(c + 1)
     for at in late:
         send_late(*at)
@@ -447,11 +455,9 @@
     range_rows = rows * parts
     ranges = DOC_MAX // range_rows
     chunks = KVH // ranges
-    units = 2 * chunks
+    units = chunks
     columns = wide // (ranges * units)
     total = columns // HD * rows
-    window = lax.axis_index("blk") // ranges
-    starts = (jnp.cumsum(doc_lengths) - doc_lengths - window * DOC_MAX).astype(jnp.int32)
     f32, bf16 = jnp.float32, jnp.bfloat16
     anywhere = pl.BlockSpec(memory_space=pl.ANY)
     vmem, dma = pltpu.VMEM, pltpu.SemaphoreType.DMA
@@ -511,7 +517,7 @@
             bytes_accessed=7 * rows * wide * 2,
             transcendentals=total * DOC_MAX * ranges * chunks // 2,
         ),
-    )(starts, query, key, value, output, out_grad, (lse * LOG2E).T, block_keep)
+    )(doc_lengths, query, key, value, output, out_grad, (lse * LOG2E).T, block_keep)
 
 
 def solution(mesh):

time: 117 us -> 113 us (0.966)
  Pallas kernels: 109 us -> 106 us
  other arithmetic: 3.37 us -> 1.38 us
    pallas_call x1, Pallas kernels: 109 us -> 106 us  [shards(): pl.pallas_call(functools.partial(whole_kernel, ranges, parts), out_shape=...]
where the time goes in v5:
time: 113 us; the launch traced here: 112 us
  Pallas kernels  106 us (94%)
  local copies, waits for them, and re-layouts  4.56 us (4%)
  other arithmetic  1.38 us (1%)
    pallas_call x1, Pallas kernels, shards(): pl.pallas_call(functools.partial(whole_kernel, ranges, parts), out_shape=...  106 us
    unnamed x7, local copies, waits for them, and re-layouts  4.56 us

profile of v5, /device:TPU:0, one launch (start us, length us, event | category | flops | bytes accessed | tf_op | source)
XLA Modules:
  0.0 112.4 jit_solution(2140621674330579465)
XLA Ops:
  0.6 1.4 %multiply_bitcast_fusion.lse_t = f32[64,128]{1,0:T(8,128)} fusion(f32[128,64]{0,1:T(8,128)} %param.13), kind=kLoop, calls=%fused_computation | loop fusion | flops 8192 | bytes 65536 | tf_op jit(solution)/shard_map/transpose | solution.py:520
  2.0 105.8 %shard_map.103 = (bf16[128,8192]{1,0:T(8,128)(2,1)}, bf16[128,1024]{1,0:T(8,128)(2,1)}, bf16[128,1024]{1,0:T(8,128)(2,1)}) custom-call(s32[3]{0:T(128)} %lengths.1, bf16[128,8192]{1,0:T(8,128)(2,1)} %query.1, bf16[128,1024]{1,0:T(8,128)(2,1)} %key.1, bf16[128,1024]{1,0:T(8,128)(2,1)} %value.1, bf16[128,8192]{1,0:T(8,128)(2,1)} %output.1, ...), custom_call_target="tpu_custom_call" | custom-call | flops 10737418240 | bytes 14680064 | tf_op jit(solution)/shard_map/pallas_call | solution.py:465
  107.8 0.0 copy-start.1
  107.8 0.0 copy-start
  107.8 3.2 %copy.14 = bf16[128,8192]{1,0:T(8,128)(2,1)} copy(bf16[128,8192]{1,0:T(8,128)(2,1)} %get-tuple-element.6) | data formatting | bytes 4194304
  111.0 0.0 copy-done.1
  111.0 0.7 copy.15
  111.7 0.0 copy-done
  111.7 0.7 copy.16
Async XLA Ops:
  107.8 3.2 %copy-start.1 = (bf16[128,1024]{1,0:T(8,128)(2,1)S(1)}, bf16[128,1024]{1,0:T(8,128)(2,1)}, u32[]{:S(2)}) copy-start(bf16[128,1024]{1,0:T(8,128)(2,1)} %get-tuple-element.7) | copy-start | bytes 786436
  107.8 3.9 %copy-start = (bf16[128,1024]{1,0:T(8,128)(2,1)S(1)}, bf16[128,1024]{1,0:T(8,128)(2,1)}, u32[]{:S(2)}) copy-start(bf16[128,1024]{1,0:T(8,128)(2,1)} %get-tuple-element.8) | copy-start | bytes 786436

commit v6 on v5

--- a/solution.py
+++ b/solution.py
@@ -165,10 +165,11 @@
         for copy in copies:
             copy.wait()
 
-    kv_moves = [kv_sends(c) for c in range(chunks)]
+    kv_moves = [kv_sends(0)]
     keep_moves = sends(2 * chunks + 2 * units + 1, lambda r: block_keep, keep_in.at[mine])
     qg_moves = [qg_sends(0)] + [None] * (units - 1)
     wait(kv_moves[0])
+    kv_moves += [kv_sends(c) for c in range(1, chunks)]
     gather(0)
     for c in range(chunks):
         for z in range(1, parts):

time: 113 us -> 113 us (level)
  no operation moved by 1% of the time
where the time goes in v6:
time: 113 us; the launch traced here: 112 us
  Pallas kernels  106 us (94%)
  local copies, waits for them, and re-layouts  4.56 us (4%)
  other arithmetic  1.38 us (1%)
    pallas_call x1, Pallas kernels, shards(): pl.pallas_call(functools.partial(whole_kernel, ranges, parts), out_shape=...  106 us
    unnamed x7, local copies, waits for them, and re-layouts  4.56 us

profile of v6, /device:TPU:0, one launch (start us, length us, event | category | flops | bytes accessed | tf_op | source)
XLA Modules:
  0.0 112.4 jit_solution(2843653579464865380)
XLA Ops:
  0.6 1.4 %multiply_bitcast_fusion.lse_t = f32[64,128]{1,0:T(8,128)} fusion(f32[128,64]{0,1:T(8,128)} %param.13), kind=kLoop, calls=%fused_computation | loop fusion | flops 8192 | bytes 65536 | tf_op jit(solution)/shard_map/transpose | solution.py:521
  2.0 105.8 %shard_map.103 = (bf16[128,8192]{1,0:T(8,128)(2,1)}, bf16[128,1024]{1,0:T(8,128)(2,1)}, bf16[128,1024]{1,0:T(8,128)(2,1)}) custom-call(s32[3]{0:T(128)} %lengths.1, bf16[128,8192]{1,0:T(8,128)(2,1)} %query.1, bf16[128,1024]{1,0:T(8,128)(2,1)} %key.1, bf16[128,1024]{1,0:T(8,128)(2,1)} %value.1, bf16[128,8192]{1,0:T(8,128)(2,1)} %output.1, ...), custom_call_target="tpu_custom_call" | custom-call | flops 10737418240 | bytes 14680064 | tf_op jit(solution)/shard_map/pallas_call | solution.py:466
  107.8 0.0 copy-start.1
  107.8 0.0 copy-start
  107.8 3.2 %copy.14 = bf16[128,8192]{1,0:T(8,128)(2,1)} copy(bf16[128,8192]{1,0:T(8,128)(2,1)} %get-tuple-element.6) | data formatting | bytes 4194304
  111.0 0.0 copy-done.1
  111.0 0.7 copy.15
  111.7 0.0 copy-done
  111.7 0.7 copy.16
Async XLA Ops:
  107.8 3.2 %copy-start.1 = (bf16[128,1024]{1,0:T(8,128)(2,1)S(1)}, bf16[128,1024]{1,0:T(8,128)(2,1)}, u32[]{:S(2)}) copy-start(bf16[128,1024]{1,0:T(8,128)(2,1)} %get-tuple-element.7) | copy-start | bytes 786436
  107.8 3.9 %copy-start = (bf16[128,1024]{1,0:T(8,128)(2,1)S(1)}, bf16[128,1024]{1,0:T(8,128)(2,1)}, u32[]{:S(2)}) copy-start(bf16[128,1024]{1,0:T(8,128)(2,1)} %get-tuple-element.8) | copy-start | bytes 786436
